TPU v7x, 256 devices: a whole 4x4x8 slice. The times are simulated.
256 devices in a mesh: lat: 64 (over z, y, core), lon: 4 (over x).
Axes of the slice: x: 4, y: 4, z: 8, core: 2. Of those that a mesh axis runs over, the one named last changes fastest.
Arguments:
- field: bfloat16 [512, 1440, 256], P('lat', 'lon'), may hold values from -6 to 6
- cotangent: bfloat16 [512, 1440, 256], P('lat', 'lon'), may hold values from -0.118585412 to 0.118585412
- legendre: bfloat16 [384, 512, 384], P('lat'), may hold values from -0.25 to 0.25
- quad_weight: float32 [512], P('lat'), may hold values from 0.25 to 2
- order_slots: int32 [384], replicated, may hold values from 0 to 383, as said below
- support_blocks: int32 [64, 3], P('lat'), may hold values from 0 to 63, as said below
- filter_values: bfloat16 [3, 512, 3, 8], P(None, 'lat'), may hold values from -1.25 to 1.25
- spectral_weight: bfloat16 [2, 256, 256], replicated, may hold values from -0.25 to 0.25
- disco_weight: bfloat16 [3, 256, 256], replicated, may hold values from -0.21875 to 0.21875
Outputs:
- output: bfloat16 [512, 1440, 256], P('lat', 'lon')
- grad_spectral: float32 [2, 256, 256], replicated
- grad_disco: float32 [3, 256, 256], replicated
Inputs may be any that keep to these rules, and one draw needn't show every extreme that they name: order_slots holds every order from 0 to 383 exactly once; the first slot of each block of 384 // 64 slots holds an order below 64. `support_blocks`: slot 0 of row block b names b itself; slots 1 and 2 name b - 1, b or b + 1.
All inputs are finite; a program needn't handle non-finite values.
Results may differ from a plain program's by a relative error of at most 0.015.
Values may be sent and summed in bfloat16 or wider, within the bound.
No kernel may reach another device: no remote copies, remote signals or barrier semaphores. Data moves between devices by JAX's collectives and lax.ppermute only.
A program may use at most 128 MiB of HBM per device.

v0:
```python
import jax
import jax.numpy as jnp
from jax import lax
from jax.sharding import PartitionSpec as P


def padded(value, sides, width, wrap):
    for axis, dim in sides:
        size, length = (lax.axis_size(axis), value.shape[dim])
        up = [(i, (i + 1) % size) for i in range(size if wrap else size - 1)]
        down = [(j, i) for i, j in up]
        last = lax.slice_in_dim(value, length - width, length, axis=dim)
        leading = lax.slice_in_dim(value, 0, width, axis=dim)
        before = lax.ppermute(last, axis, up)
        after = lax.ppermute(leading, axis, down)
        value = jnp.concatenate([before, value, after], axis=dim)
    return value


def fourier_tables(order_slots, nlon):
    column = jnp.arange(nlon, dtype=jnp.int32)
    phase = column[:, None] * order_slots[None, :] % nlon
    angle = phase.astype(jnp.float32) * (2.0 * jnp.pi / nlon)
    cosine = jnp.cos(angle)
    sine = jnp.sin(angle)
    factor = jnp.where(order_slots == 0, 1.0, 2.0).astype(jnp.float32)[None, :]
    analysis_table = jnp.concatenate([cosine / nlon, -sine / nlon], axis=1).astype(jnp.bfloat16)
    synthesis_table = jnp.concatenate([factor * cosine, -factor * sine], axis=1).astype(
        jnp.bfloat16
    )
    return (analysis_table, synthesis_table)


def outer_sum(left, right):
    return lax.dot_general(
        left, right, (((0,), (0,)), ((), ())), preferred_element_type=jnp.float32
    )


def complex_mix(real_part, imag_part, w_real, w_imag):
    out_real = jnp.dot(real_part, w_real, preferred_element_type=jnp.float32) - jnp.dot(
        imag_part, w_imag, preferred_element_type=jnp.float32
    )
    out_imag = jnp.dot(real_part, w_imag, preferred_element_type=jnp.float32) + jnp.dot(
        imag_part, w_real, preferred_element_type=jnp.float32
    )
    return (out_real, out_imag)


def to_degrees(values):
    return lax.all_to_all(values, "lon", split_axis=1, concat_axis=3, tiled=True)


def local(
    field,
    cotangent,
    legendre,
    quad_weight,
    order_slots,
    support_blocks,
    filter_values,
    spectral_weight,
    disco_weight,
):
    f32 = jnp.float32
    bf16 = jnp.bfloat16
    lat_rows, lon_cols, channels = field.shape
    nlon = lon_cols * lax.axis_size("lon")
    slots_dev, nlat, degrees = legendre.shape
    quarter = channels // lax.axis_size("lon")
    mmax = order_slots.shape[0]
    lat_pos = lax.axis_index("lat")
    analysis_table, synthesis_table = fourier_tables(order_slots, nlon)
    own_orders = lax.dynamic_slice_in_dim(order_slots, lat_pos * slots_dev, slots_dev)
    degree_mask = (jnp.arange(degrees, dtype=jnp.int32)[None, :] >= own_orders[:, None]).astype(f32)

    def longitude_transform(values, table):
        slabs = lax.all_to_all(values, "lon", split_axis=2, concat_axis=1, tiled=True)
        return jnp.einsum("ajc,jq->aqc", slabs, table, preferred_element_type=f32)

    def legendre_forward(spectrum):
        shaped = spectrum.reshape(lat_rows, 2, mmax, -1).astype(bf16)
        coeffs = jnp.einsum(
            "kal,arkc->klrc",
            legendre,
            lax.all_to_all(shaped, "lat", split_axis=2, concat_axis=0, tiled=True),
            preferred_element_type=f32,
        )
        return (coeffs * degree_mask[:, :, None, None]).astype(bf16)

    spectrum = longitude_transform(field, analysis_table) * quad_weight[:, None, None]
    coeffs = legendre_forward(spectrum)
    degree_coeffs = to_degrees(coeffs)
    real_part = degree_coeffs[:, :, 0].reshape(-1, channels)
    imag_part = degree_coeffs[:, :, 1].reshape(-1, channels)
    out_real, out_imag = complex_mix(real_part, imag_part, spectral_weight[0], spectral_weight[1])
    mixed_degrees = jnp.stack(
        [out_real.reshape(slots_dev, -1, channels), out_imag.reshape(slots_dev, -1, channels)],
        axis=2,
    ).astype(bf16)
    mixed = lax.all_to_all(mixed_degrees, "lon", split_axis=3, concat_axis=1, tiled=True)
    masked = mixed * degree_mask.astype(bf16)[:, :, None, None]
    grid_spectrum = jnp.einsum(
        "kal,klrc->arkc", legendre, masked, preferred_element_type=f32
    ).astype(bf16)
    lat_spectrum = lax.all_to_all(grid_spectrum, "lat", split_axis=0, concat_axis=2, tiled=True)
    partial_field = jnp.einsum(
        "aqc,jq->ajc",
        lat_spectrum.reshape(lat_rows, 2 * mmax, quarter),
        synthesis_table,
        preferred_element_type=f32,
    ).astype(bf16)
    spectral_out = lax.all_to_all(partial_field, "lon", split_axis=1, concat_axis=2, tiled=True)
    rimmed = padded(field, (("lon", 1),), 1, True)
    extended = padded(rimmed, (("lat", 0),), lat_rows, False)
    picks = support_blocks[0] - lat_pos + 1
    onehot = (picks[:, None] == jnp.arange(3, dtype=jnp.int32)[None, :]).astype(f32)
    operator = (
        jnp.einsum("tasb,sq->taqb", filter_values.astype(f32), onehot)
        .reshape(3, lat_rows, 3 * lat_rows)
        .astype(bf16)
    )
    responses = []
    disco_sum = jnp.zeros((lat_rows * lon_cols, channels), f32)
    for tap in range(3):
        window = extended[:, tap : tap + lon_cols]
        response = jnp.einsum(
            "ab,boc->aoc", operator[tap], window, preferred_element_type=f32
        ).astype(bf16)
        responses.append(response)
        disco_sum = disco_sum + jnp.dot(
            response.reshape(-1, channels), disco_weight[tap], preferred_element_type=f32
        )
    pre_act = spectral_out.astype(f32) + disco_sum.reshape(lat_rows, lon_cols, channels)
    activated, pullback = jax.vjp(jax.nn.gelu, pre_act)
    output = (field.astype(f32) + activated).astype(bf16)
    (grad_pre,) = pullback(cotangent.astype(f32))
    grad_pre = grad_pre.astype(bf16)
    flat_grad = grad_pre.reshape(-1, channels)
    disco_terms = jnp.stack(
        [outer_sum(response.reshape(-1, channels), flat_grad) for response in responses]
    )
    grad_disco = lax.psum(disco_terms, ("lat", "lon"))
    grad_grid = longitude_transform(grad_pre, synthesis_table)
    grad_coeffs = legendre_forward(grad_grid)
    degree_grad = to_degrees(grad_coeffs)
    grad_real = degree_grad[:, :, 0].reshape(-1, channels)
    grad_imag = degree_grad[:, :, 1].reshape(-1, channels)
    g_real = outer_sum(real_part, grad_real) + outer_sum(imag_part, grad_imag)
    g_imag = outer_sum(real_part, grad_imag) - outer_sum(imag_part, grad_real)
    grad_spectral = lax.psum(jnp.stack([g_real, g_imag]), ("lat", "lon"))
    return (output, grad_spectral, grad_disco)


def solution(mesh):
    placed = (
        P("lat", "lon", None),
        P("lat", "lon", None),
        P("lat", None, None),
        P("lat"),
        P(),
        P("lat", None),
        P(None, "lat", None, None),
        P(),
        P(),
    )
    return jax.shard_map(
        local,
        mesh=mesh,
        in_specs=placed,
        out_specs=(P("lat", "lon", None), P(), P()),
        check_vma=False,
    )
```

profile of v0, /device:TPU:1, one launch (start us, length us, event | category | flops | bytes accessed | tf_op | source)
XLA Modules:
  0.0 652.6 jit_solution(4257099778303445396)
XLA Ops:
  10.2 5.0 all-to-all-start
  15.2 11.3 %multiply_convert_fusion.3 = (bf16[1440,384]{1,0:T(8,128)(2,1)}, bf16[1440,384]{1,0:T(8,128)(2,1)S(1)}, bf16[1440,384]{1,0:T(8,128)(2,1)}, bf16[1440,384]{1,0:T(8,128)(2,1)}) fusion(s32[384]{0:T(512)S(1)} %copy-done.16, f32[384]{0:T(512)S(1)} %get-tuple-element.27, f32[384]{0:T(512)S(1)} %get-tuple-element.28), kind=kLoop, calls=%fused_computation.41 | loop fusion | flops 9953280 | bytes 4428288 | tf_op jit(solution)/shard_map/convert.9
  26.5 7.0 %all-to-all-done = bf16[8,360,256]{1,0,2:T(8,128)(2,1)} async-done(((bf16[8,360,256]{1,0,2:T(8,128)(2,1)}), bf16[8,360,256]{1,0,2:T(8,128)(2,1)}, u32[]{:S(2)}, u32[]{:S(2)}) %all-to-all-start) | async-done | bytes 1474592 | tf_op jit(solution)/shard_map/all_to_all | solution.py:78
  37.3 4.0 all_to_all.112
  45.7 3.8 copy.151
  49.5 3.8 reshape.145
  53.3 15.4 %all-to-all-start.1 = ((bf16[64,2,3072]{2,1,0:T(2,128)(2,1)}), bf16[64,2,3072]{2,1,0:T(2,128)(2,1)S(1)}, u32[]{:S(2)}, u32[]{:S(2)}) async-start(bf16[64,2,3072]{2,1,0:T(2,128)(2,1)} %reshape.145), calls=%async_computation.1 | async-start | bytes 1572864 | tf_op jit(solution)/shard_map/all_to_all | solution.py:86
  72.4 19.0 %all-to-all-done.1 = bf16[64,2,3072]{2,1,0:T(2,128)(2,1)S(1)} async-done(((bf16[64,2,3072]{2,1,0:T(2,128)(2,1)}), bf16[64,2,3072]{2,1,0:T(2,128)(2,1)S(1)}, u32[]{:S(2)}, u32[]{:S(2)}) %all-to-all-start.1) | async-done | bytes 786464 | tf_op jit(solution)/shard_map/all_to_all | solution.py:86
  136.5 4.4 pad_maximum_fusion.4
  140.9 4.5 all-to-all-start.3
  145.6 11.5 %all-to-all-done.3 = bf16[6,96,2,256]{1,2,0,3:T(2,128)(2,1)} async-done(((bf16[6,96,2,256]{1,2,0,3:T(2,128)(2,1)}), bf16[6,96,2,256]{1,2,0,3:T(2,128)(2,1)}, u32[]{:S(2)}, u32[]{:S(2)}) %all-to-all-start.3) | async-done | bytes 589856 | tf_op jit(solution)/shard_map/all_to_all | solution.py:101
  165.1 4.8 copy.163
  169.9 4.8 reshape.149
  174.7 7.3 %all-to-all-start.4 = ((bf16[64,2,3072]{2,1,0:T(2,128)(2,1)}), bf16[64,2,3072]{2,1,0:T(2,128)(2,1)}, u32[]{:S(2)}, u32[]{:S(2)}) async-start(bf16[64,2,3072]{2,1,0:T(2,128)(2,1)} %reshape.149), calls=%async_computation.4 | async-start | bytes 1572864 | tf_op jit(solution)/shard_map/all_to_all | solution.py:106
  193.5 10.9 %all-to-all-done.4 = bf16[64,2,3072]{2,1,0:T(2,128)(2,1)} async-done(((bf16[64,2,3072]{2,1,0:T(2,128)(2,1)}), bf16[64,2,3072]{2,1,0:T(2,128)(2,1)}, u32[]{:S(2)}, u32[]{:S(2)}) %all-to-all-start.4) | async-done | bytes 786464 | tf_op jit(solution)/shard_map/all_to_all | solution.py:106
  204.4 4.7 reshape.150
  219.5 4.8 copy.167
  224.3 4.9 reshape.151
  229.2 4.7 all-to-all-start.5
  239.5 13.2 %all-to-all-done.5 = bf16[4,2,92160]{2,1,0:T(2,128)(2,1)} async-done(((bf16[4,2,92160]{2,1,0:T(2,128)(2,1)}), bf16[4,2,92160]{2,1,0:T(2,128)(2,1)}, u32[]{:S(2)}, u32[]{:S(2)}) %all-to-all-start.5) | async-done | bytes 1474592 | tf_op jit(solution)/shard_map/all_to_all | solution.py:113
  252.7 4.8 reshape.152
  257.5 5.2 copy.168
  266.4 5.9 fusion.8
  275.2 22.4 %all_to_all.150 = bf16[8,360,256]{1,0,2:T(8,128)(2,1)S(1)} all-to-all(bf16[8,360,256]{1,0,2:T(8,128)(2,1)} %copy.177), channel_id=1, replica_groups=mesh['lat'=64,'lon'=4] {'lon'}, dimensions={2} | all-to-all | bytes 2949120 | tf_op jit(solution)/shard_map/all_to_all | solution.py:78
  300.0 4.0 all_to_all.132
  311.2 3.8 copy.180
  318.8 9.3 %all-to-all-start.7 = ((bf16[64,2,3072]{2,1,0:T(2,128)(2,1)}), bf16[64,2,3072]{2,1,0:T(2,128)(2,1)}, u32[]{:S(2)}, u32[]{:S(2)}) async-start(bf16[64,2,3072]{2,1,0:T(2,128)(2,1)} %reshape.153), calls=%async_computation.7 | async-start | bytes 1572864 | tf_op jit(solution)/shard_map/all_to_all | solution.py:86
  332.3 18.3 %all-to-all-done.7 = bf16[64,2,3072]{2,1,0:T(2,128)(2,1)} async-done(((bf16[64,2,3072]{2,1,0:T(2,128)(2,1)}), bf16[64,2,3072]{2,1,0:T(2,128)(2,1)}, u32[]{:S(2)}, u32[]{:S(2)}) %all-to-all-start.7) | async-done | bytes 786464 | tf_op jit(solution)/shard_map/all_to_all | solution.py:86
  357.2 4.6 copy.184
  364.5 4.2 all-to-all-start.8
  372.3 5.7 all-to-all-done.8
  388.5 253.9 %all-reduce.3.cloned.1.call-done = (f32[2,256,256]{2,1,0:T(8,128)}, f32[3,256,256]{2,1,0:T(8,128)}) async-done(((f32[2,256,256]{2,1,0:T(8,128)}, f32[3,256,256]{2,1,0:T(8,128)}), (f32[2,256,256]{2,1,0:T(8,128)}, f32[3,256,256]{2,1,0:T(8,128)})) %all-reduce.3.cloned.1.call-update) | async-done | bytes 1310736 | tf_op jit(solution)/shard_map/psum | solution.py:151
  (129 shorter events, 145.5 us)
Async XLA Ops:
  7.2 86.1 %copy-start = (bf16[6,512,384]{2,1,0:T(8,128)(2,1)S(1)}, bf16[6,512,384]{2,1,0:T(8,128)(2,1)}, u32[]{:S(2)}) copy-start(bf16[6,512,384]{2,1,0:T(8,128)(2,1)} %param.11) | copy-start | bytes 7077892
  10.2 5.0 copy-start.16
  10.2 23.3 %all-to-all-start = ((bf16[8,360,256]{1,0,2:T(8,128)(2,1)}), bf16[8,360,256]{1,0,2:T(8,128)(2,1)}, u32[]{:S(2)}, u32[]{:S(2)}) async-start(bf16[8,360,256]{1,0,2:T(8,128)(2,1)} %copy.148), calls=%async_computation | async-start | bytes 3145728 | tf_op jit(solution)/shard_map/all_to_all | solution.py:78
  41.3 3.1 copy-start.17
  53.3 38.2 %all-to-all-start.1 = ((bf16[64,2,3072]{2,1,0:T(2,128)(2,1)}), bf16[64,2,3072]{2,1,0:T(2,128)(2,1)S(1)}, u32[]{:S(2)}, u32[]{:S(2)}) async-start(bf16[64,2,3072]{2,1,0:T(2,128)(2,1)} %reshape.145), calls=%async_computation.1 | async-start | bytes 1572864 | tf_op jit(solution)/shard_map/all_to_all | solution.py:86
  69.5 35.3 %collective-permute-start = (bf16[8,1,256]{2,0,1:T(8,128)(2,1)S(1)}, bf16[8,1,256]{2,0,1:T(8,128)(2,1)}, u32[]{:S(2)}, u32[]{:S(2)}) collective-permute-start(bf16[8,1,256]{2,0,1:T(8,128)(2,1)S(1)} %copy.233), channel_id=1, source_target_pairs={{0,1},{1,2},{2,3},{3,0},{4,5},{5,6},{6,7},{7,4},{8,9},{9,10},{10,1... | collective-permute-start | bytes 12296 | tf_op jit(solution)/shard_map/ppermute | solution.py:14
  69.9 39.0 %collective-permute-start.1 = (bf16[8,1,256]{2,0,1:T(8,128)(2,1)S(1)}, bf16[8,1,256]{2,0,1:T(8,128)(2,1)}, u32[]{:S(2)}, u32[]{:S(2)}) collective-permute-start(bf16[8,1,256]{2,0,1:T(8,128)(2,1)S(1)} %copy.234), channel_id=1, source_target_pairs={{1,0},{2,1},{3,2},{0,3},{5,4},{6,5},{7,6},{4,7},{9,8},{10,9},{11,1... | collective-permute-start | bytes 12296 | tf_op jit(solution)/shard_map/ppermute | solution.py:15
  72.4 20.9 %copy-start.14 = (f32[6,384]{1,0:T(8,128)}, f32[6,384]{1,0:T(8,128)S(1)}, u32[]{:S(2)}) copy-start(f32[6,384]{1,0:T(8,128)S(1)} %get-tuple-element.30) | copy-start | bytes 27652
  101.3 14.9 %all-to-all-start.2 = ((bf16[4,2,36864]{2,1,0:T(2,128)(2,1)}), bf16[4,2,36864]{2,1,0:T(2,128)(2,1)S(1)}, u32[]{:S(2)}, u32[]{:S(2)}) async-start(bf16[4,2,36864]{2,1,0:T(2,128)(2,1)} %reshape.147), calls=%async_computation.2 | async-start | bytes 1179648 | tf_op jit(solution)/shard_map/all_to_all | solution.py:51
  110.2 72.0 %collective-permute-start.3 = (bf16[8,362,256]{2,0,1:T(8,128)(2,1)}, bf16[8,362,256]{2,0,1:T(8,128)(2,1)}, u32[]{:S(2)}, u32[]{:S(2)}) collective-permute-start(bf16[8,362,256]{2,0,1:T(8,128)(2,1)} %constant_dynamic-update-slice_fusion), channel_id=1, source_target_pairs={{4,0},{8,4},{12,8},{16,12},{20,16},{24,20},{28,24},{32,28},{36,32}... | collective-permute-start | bytes 4448264 | tf_op jit(solution)/shard_map/ppermute | solution.py:15
  113.1 69.2 %collective-permute-start.2 = (bf16[8,362,256]{2,0,1:T(8,128)(2,1)}, bf16[8,362,256]{2,0,1:T(8,128)(2,1)}, u32[]{:S(2)}, u32[]{:S(2)}) collective-permute-start(bf16[8,362,256]{2,0,1:T(8,128)(2,1)} %constant_dynamic-update-slice_fusion), channel_id=1, source_target_pairs={{0,4},{4,8},{8,12},{12,16},{16,20},{20,24},{24,28},{28,32},{32,36}... | collective-permute-start | bytes 4448264 | tf_op jit(solution)/shard_map/ppermute | solution.py:14
  124.4 3.1 copy-start.9
  124.4 3.1 copy-start.10
  136.5 8.9 %copy-start.19 = (s32[1,3]{1,0:T(1,128)S(1)}, s32[1,3]{1,0:T(1,128)}, u32[]{:S(2)}) copy-start(s32[1,3]{1,0:T(1,128)} %param.14) | copy-start | bytes 40
  136.5 8.9 %copy-start.18 = (bf16[3,8,3,8]{3,1,2,0:T(8,128)(2,1)S(1)}, bf16[3,8,3,8]{3,1,2,0:T(8,128)(2,1)}, u32[]{:S(2)}) copy-start(bf16[3,8,3,8]{3,1,2,0:T(8,128)(2,1)} %param.15) | copy-start | bytes 3460
  140.9 16.2 %all-to-all-start.3 = ((bf16[6,96,2,256]{1,2,0,3:T(2,128)(2,1)}), bf16[6,96,2,256]{1,2,0,3:T(2,128)(2,1)}, u32[]{:S(2)}, u32[]{:S(2)}) async-start(bf16[6,96,2,256]{1,2,0,3:T(2,128)(2,1)} %pad_maximum_fusion.4), calls=%async_computation.3 | async-start | bytes 1572864 | tf_op jit(solution)/shard_map/all_to_all | solution.py:101
  174.7 29.8 %all-to-all-start.4 = ((bf16[64,2,3072]{2,1,0:T(2,128)(2,1)}), bf16[64,2,3072]{2,1,0:T(2,128)(2,1)}, u32[]{:S(2)}, u32[]{:S(2)}) async-start(bf16[64,2,3072]{2,1,0:T(2,128)(2,1)} %reshape.149), calls=%async_computation.4 | async-start | bytes 1572864 | tf_op jit(solution)/shard_map/all_to_all | solution.py:106
  185.6 2.7 copy-start.3
  188.3 2.6 copy-start.4
  229.2 4.7 copy-start.12
  229.2 23.5 %all-to-all-start.5 = ((bf16[4,2,92160]{2,1,0:T(2,128)(2,1)}), bf16[4,2,92160]{2,1,0:T(2,128)(2,1)}, u32[]{:S(2)}, u32[]{:S(2)}) async-start(bf16[4,2,92160]{2,1,0:T(2,128)(2,1)} %reshape.151), calls=%async_computation.5 | async-start | bytes 2949120 | tf_op jit(solution)/shard_map/all_to_all | solution.py:113
  233.9 2.0 copy-start.1
  236.0 1.4 copy-start.2
  318.8 31.8 %all-to-all-start.7 = ((bf16[64,2,3072]{2,1,0:T(2,128)(2,1)}), bf16[64,2,3072]{2,1,0:T(2,128)(2,1)}, u32[]{:S(2)}, u32[]{:S(2)}) async-start(bf16[64,2,3072]{2,1,0:T(2,128)(2,1)} %reshape.153), calls=%async_computation.7 | async-start | bytes 1572864 | tf_op jit(solution)/shard_map/all_to_all | solution.py:86
  328.1 2.7 copy-start.6
  328.1 2.7 copy-start.7
  332.3 21.9 %copy-start.15 = (f32[6,384]{1,0:T(8,128)S(1)}, f32[6,384]{1,0:T(8,128)}, u32[]{:S(2)}) copy-start(f32[6,384]{1,0:T(8,128)} %copy-done.14) | copy-start | bytes 27652
  364.5 13.5 %all-to-all-start.8 = ((bf16[4,2,36864]{2,1,0:T(2,128)(2,1)}), bf16[4,2,36864]{2,1,0:T(2,128)(2,1)}, u32[]{:S(2)}, u32[]{:S(2)}) async-start(bf16[4,2,36864]{2,1,0:T(2,128)(2,1)} %reshape.155), calls=%async_computation.8 | async-start | bytes 1179648 | tf_op jit(solution)/shard_map/all_to_all | solution.py:51
  368.6 273.8 %all-reduce.3.cloned.1.call-start = ((), (), s32[]{:S(2)}) async-start(), calls=%async_computation.9 | async-start | bytes 2621440 | tf_op jit(solution)/shard_map/psum | solution.py:151
  368.7 2.6 copy-start.13
  384.3 2.7 copy-start.8
  642.4 1.9 copy-start.11
  (1 other events, 1.1 us)
Sparse Core Ops, SparseCore 0:
  388.6 253.7 all-reduce.2
where the time goes:
time: 664 us; the launch traced here: 653 us
  waiting for transfers between devices  340 us (51%)
  local copies, waits for them, and re-layouts  142 us (21%)
  starting transfers between devices  62.6 us (9%)
  matrix products  42.4 us (6%)
  other arithmetic  28.3 us (4%)
  blocking collectives  22.4 us (3%)
  between operations  15 us (2%)
    psum x1, waiting for transfers between devices, local(): grad_spectral = lax.psum(jnp.stack([g_real, g_imag]), ('lat', 'lon'))  254 us
    unnamed x61, local copies, waits for them, and re-layouts  55.9 us
    all_to_all x2, waiting for transfers between devices, legendre_forward(): lax.all_to_all(shaped, 'lat', split_axis=2, concat_axis=0, tiled=True)  37.3 us
    all_to_all x2, starting transfers between devices, legendre_forward(): lax.all_to_all(shaped, 'lat', split_axis=2, concat_axis=0, tiled=True)  24.7 us
    all_to_all x1, blocking collectives, longitude_transform(): lax.all_to_all(values, 'lon', split_axis=2, concat_axis=1, tiled=True)  22.4 us
    all_to_all x4, local copies, waits for them, and re-layouts, longitude_transform(): lax.all_to_all(values, 'lon', split_axis=2, concat_axis=1, tiled=True)  14.2 us
  transfers between devices with their start and end apart: 13, of which 8 were waited for; matrix products, arithmetic and copies ran while one was open for 14% of the time, Pallas kernels for 0%

commit v1 on v0

v1 whole, which is shorter than its diff:
```python
import functools
import math

import jax
import jax.numpy as jnp
from jax import lax
from jax.experimental import pallas as pl
from jax.experimental.pallas import tpu as pltpu
from jax.sharding import PartitionSpec as P

F32 = jnp.float32
BF16 = jnp.bfloat16
LANES = 128
HALF = LANES // 2
GELU_SCALE = math.sqrt(2.0 / math.pi)
GELU_CUBE = 0.044715


def kernel_call(kernel, grid, in_specs, out_specs, out_shape, flops, scratch=(), limit=56):
    leaves = jax.tree.leaves(out_shape)
    size = sum(leaf.size * leaf.dtype.itemsize for leaf in leaves)
    return pl.pallas_call(
        kernel,
        grid=grid,
        in_specs=in_specs,
        out_specs=out_specs,
        out_shape=out_shape,
        scratch_shapes=list(scratch),
        compiler_params=pltpu.CompilerParams(
            dimension_semantics=("arbitrary",) * len(grid), vmem_limit_bytes=limit << 20
        ),
        cost_estimate=pl.CostEstimate(flops=flops, bytes_accessed=3 * size, transcendentals=0),
    )


def low_lanes(rows):
    return lax.broadcasted_iota(jnp.int32, (rows, LANES), 1) < HALF


def swap(value):
    return pltpu.roll(value, HALF, 1)


def exchange(low, first, second):
    return (jnp.where(low, first, swap(second)), jnp.where(low, swap(first), second))


def pack_kernel(field_ref, out_ref):
    low = low_lanes(field_ref.shape[1])
    for tile in range(field_ref.shape[2] // LANES):
        lanes = slice(tile * LANES, (tile + 1) * LANES)
        first, second = exchange(
            low, field_ref[0, :, lanes].astype(F32), field_ref[1, :, lanes].astype(F32)
        )
        out_ref[2 * tile] = first.astype(BF16)
        out_ref[2 * tile + 1] = second.astype(BF16)


def pack(field):
    rows, cols, channels = field.shape
    parts = channels // HALF
    return kernel_call(
        pack_kernel,
        (rows // 2,),
        [pl.BlockSpec((2, cols, channels), lambda i: (i, 0, 0))],
        pl.BlockSpec((parts, cols, LANES), lambda i: (0, 0, i)),
        jax.ShapeDtypeStruct((parts, cols, rows * HALF), BF16),
        0,
    )(field)


def analysis_kernel(pairs, table_ref, slab_ref, weight_ref, out_ref, wide_ref):
    rows = table_ref.shape[0]
    for two in range(pairs // 2):
        lanes = slice(two * 2 * LANES, (two + 1) * 2 * LANES)
        part = jnp.dot(table_ref[...], slab_ref[:, lanes], preferred_element_type=F32)
        part = part * weight_ref[:, lanes]
        wide_ref[pl.ds(2 * two, rows, stride=pairs), :] = part[:, :LANES]
        wide_ref[pl.ds(2 * two + 1, rows, stride=pairs), :] = part[:, LANES:]
    out_ref[...] = wide_ref[...].astype(BF16)


def analysis(table, slabs, weight):
    coefs, nlon = table.shape
    pairs = slabs.shape[1] // LANES
    steps = 4
    rows = coefs // steps
    return kernel_call(
        functools.partial(analysis_kernel, pairs),
        (steps,),
        [
            pl.BlockSpec((rows, nlon), lambda i: (i, 0)),
            pl.BlockSpec(slabs.shape, lambda i: (0, 0)),
            pl.BlockSpec(weight.shape, lambda i: (0, 0)),
        ],
        pl.BlockSpec((rows * pairs, LANES), lambda i: (i, 0)),
        jax.ShapeDtypeStruct((coefs * pairs, LANES), BF16),
        2 * coefs * nlon * slabs.shape[1],
        [pltpu.VMEM((rows * pairs, LANES), F32)],
    )(table, slabs, weight)


def legendre_kernel(slots, pairs, blocks, leg_ref, mask_ref, spec_ref, out_ref, wide_ref, lat_ref, back_ref):
    slot = pl.program_id(0)
    low = low_lanes(blocks)
    rows = 2 * pairs
    piece = 2 * slots * pairs

    @pl.when(slot == 0)
    def _():
        wide_ref[...] = spec_ref[...].astype(F32)

    def taken(part, pair):
        return pl.ds((part * slots + slot) * pairs + pair, blocks, stride=piece)

    for pair in range(pairs):
        even, odd = exchange(low, wide_ref[taken(0, pair), :], wide_ref[taken(1, pair), :])
        lat_ref[pl.ds(2 * pair, blocks, stride=rows), :] = even
        lat_ref[pl.ds(2 * pair + 1, blocks, stride=rows), :] = odd
    leg = leg_ref[0]
    coeffs = lax.dot_general(
        lat_ref[...].astype(BF16), leg, (((0,), (0,)), ((), ())), preferred_element_type=F32
    )
    coeffs = (coeffs * mask_ref[0]).astype(BF16)
    lat_ref[...] = lax.dot_general(
        leg, coeffs, (((1,), (1,)), ((), ())), preferred_element_type=F32
    )
    for pair in range(pairs):
        real, imag = exchange(
            low,
            lat_ref[pl.ds(2 * pair, blocks, stride=rows), :],
            lat_ref[pl.ds(2 * pair + 1, blocks, stride=rows), :],
        )
        back_ref[taken(0, pair), :] = real
        back_ref[taken(1, pair), :] = imag

    @pl.when(slot == slots - 1)
    def _():
        out_ref[...] = back_ref[...].astype(BF16)


def legendre_round_trip(legendre, mask, spectrum, pairs):
    slots, nlat, degrees = legendre.shape
    blocks = nlat // (2 * pairs)
    whole = pl.BlockSpec(spectrum.shape, lambda k: (0, 0))
    return kernel_call(
        functools.partial(legendre_kernel, slots, pairs, blocks),
        (slots,),
        [
            pl.BlockSpec((1, nlat, degrees), lambda k: (k, 0, 0)),
            pl.BlockSpec((1, 1, degrees), lambda k: (k, 0, 0)),
            whole,
        ],
        whole,
        jax.ShapeDtypeStruct(spectrum.shape, BF16),
        4 * slots * nlat * degrees * LANES,
        [
            pltpu.VMEM(spectrum.shape, F32),
            pltpu.VMEM((nlat, LANES), F32),
            pltpu.VMEM(spectrum.shape, F32),
        ],
    )(legendre, mask, spectrum)


def regroup_kernel(pairs, in_ref, out_ref, wide_ref):
    wide_ref[...] = in_ref[...].astype(F32)
    for pair in range(pairs):
        out_ref[pair] = wide_ref[pl.ds(pair, out_ref.shape[1], stride=pairs), :].astype(BF16)


def regroup(rows, pairs):
    coefs = rows.shape[0] // pairs
    return kernel_call(
        functools.partial(regroup_kernel, pairs),
        (1,),
        [pl.BlockSpec(rows.shape, lambda i: (0, 0))],
        pl.BlockSpec((pairs, coefs, LANES), lambda i: (0, 0, 0)),
        jax.ShapeDtypeStruct((pairs, coefs, LANES), BF16),
        0,
        [pltpu.VMEM(rows.shape, F32)],
    )(rows)


def finish_kernel(spec_ref, table_ref, resp_ref, field_ref, cot_ref, weight_ref, out_ref, grad_ref, mix_ref):
    pair = pl.program_id(0)
    parts, _, coefs, _ = spec_ref.shape
    channels = field_ref.shape[2]
    low = low_lanes(coefs)

    @pl.when(pair == 0)
    def _():
        grad_ref[...] = jnp.zeros_like(grad_ref)

    tiles = [
        exchange(low, spec_ref[2 * i, 0].astype(F32), spec_ref[2 * i + 1, 0].astype(F32))
        for i in range(parts // 2)
    ]
    for half in range(2):
        spectrum = jnp.concatenate([tile[half] for tile in tiles], axis=1).astype(BF16)
        for part in range(2):
            mix_ref[:, part * channels : (part + 1) * channels] = jnp.dot(
                table_ref[part], spectrum, preferred_element_type=F32
            ).astype(BF16)
        for tap in range(3):
            mix_ref[:, (2 + tap) * channels : (3 + tap) * channels] = resp_ref[tap, half]
        pre = jnp.dot(mix_ref[...], weight_ref[...], preferred_element_type=F32)
        square = pre * pre
        bend = jnp.tanh(GELU_SCALE * (pre + GELU_CUBE * (square * pre)))
        activated = 0.5 * pre * (1.0 + bend)
        slope = 0.5 * (1.0 + bend) + 0.5 * pre * (1.0 - bend * bend) * (
            GELU_SCALE * (1.0 + 3.0 * GELU_CUBE * square)
        )
        out_ref[half] = (field_ref[half].astype(F32) + activated).astype(BF16)
        grad_pre = (cot_ref[half].astype(F32) * slope).astype(BF16)
        grad_ref[...] += lax.dot_general(
            mix_ref[...], grad_pre, (((0,), (0,)), ((), ())), preferred_element_type=F32
        )


def finish(spectrum, table, responses, field, cotangent, weights):
    rows, cols, channels = field.shape
    parts, pairs, coefs, _ = spectrum.shape
    pixels = pl.BlockSpec((2, cols, channels), lambda i: (i, 0, 0))
    stacked = weights.shape[0]
    return kernel_call(
        finish_kernel,
        (pairs,),
        [
            pl.BlockSpec((parts, 1, coefs, LANES), lambda i: (0, i, 0, 0)),
            pl.BlockSpec(table.shape, lambda i: (0, 0, 0)),
            pl.BlockSpec((3, 2, cols, channels), lambda i: (0, i, 0, 0)),
            pixels,
            pixels,
            pl.BlockSpec(weights.shape, lambda i: (0, 0)),
        ],
        [pixels, pl.BlockSpec((stacked, channels), lambda i: (0, 0))],
        [
            jax.ShapeDtypeStruct(field.shape, BF16),
            jax.ShapeDtypeStruct((stacked, channels), F32),
        ],
        2 * rows * cols * channels * (2 * coefs + 2 * stacked),
        [pltpu.VMEM((cols, stacked), BF16)],
    )(spectrum, table, responses, field, cotangent, weights)


def wave(column, order, shift, nlon):
    quarter = nlon // 4
    phase = (column * order).astype(F32)
    turns = jnp.floor((phase + 0.5) * (1.0 / quarter))
    rest = phase - turns * quarter
    turns = turns + shift.astype(F32)
    turns = turns - 4.0 * jnp.floor(turns * 0.25)
    odd = (turns == 1.0) | (turns == 3.0)
    angle = jnp.where(odd, quarter - rest, rest) * (2.0 * math.pi / nlon)
    square = angle * angle
    total = jnp.full_like(square, 1.0 / math.factorial(12))
    for power in (10, 8, 6, 4, 2, 0):
        total = total * square + (-1.0) ** (power // 2) / math.factorial(power)
    return jnp.where((turns == 1.0) | (turns == 2.0), -total, total)


def disco_responses(field, support_blocks, filter_values):
    rows, cols, _ = field.shape
    lat_pos, size = lax.axis_index("lat"), lax.axis_size("lat")
    up = [(i, i + 1) for i in range(size - 1)]
    down = [(j, i) for i, j in up]
    extended = jnp.concatenate(
        [lax.ppermute(field, "lat", up), field, lax.ppermute(field, "lat", down)], axis=0
    )
    lon = lax.axis_size("lon")
    east = [(i, (i + 1) % lon) for i in range(lon)]
    west = [(j, i) for i, j in east]
    before = lax.ppermute(extended[:, cols - 1 :], "lon", east)
    after = lax.ppermute(extended[:, :1], "lon", west)
    rimmed = jnp.concatenate([before, extended, after], axis=1)
    picks = support_blocks[0] - lat_pos + 1
    onehot = (picks[:, None] == jnp.arange(3, dtype=jnp.int32)[None, :]).astype(F32)
    operator = (
        jnp.einsum("tasb,sq->taqb", filter_values.astype(F32), onehot)
        .reshape(3, rows, 3 * rows)
        .astype(BF16)
    )
    return jnp.stack(
        [
            jnp.einsum(
                "ab,boc->aoc", operator[tap], rimmed[:, tap : tap + cols], preferred_element_type=F32
            ).astype(BF16)
            for tap in range(3)
        ]
    )


def sum_everywhere(terms):
    rows, channels = terms.shape
    lon, lat = lax.axis_size("lon"), lax.axis_size("lat")
    share = rows // lon
    parts = lax.all_to_all(
        terms.astype(BF16).reshape(lon, share, channels), "lon", 0, 0, tiled=True
    )
    partial = jnp.sum(parts.astype(F32), axis=0).astype(BF16)
    step = 8 * pl.cdiv(share, 8 * lat)
    padded = jnp.pad(partial, ((0, lat * step - share), (0, 0))).reshape(lat, step, channels)
    pieces = lax.all_to_all(padded, "lat", 0, 0, tiled=True)
    own = jnp.sum(pieces.astype(F32), axis=0).astype(BF16)
    gathered = lax.all_to_all(
        jnp.broadcast_to(own[None], (lat, step, channels)), "lat", 0, 0, tiled=True
    )
    mine = gathered.reshape(lat * step, channels)[:share]
    everything = lax.all_gather(mine, "lon", tiled=True)
    return everything.astype(F32)


def local(
    field,
    cotangent,
    legendre,
    quad_weight,
    order_slots,
    support_blocks,
    filter_values,
    spectral_weight,
    disco_weight,
):
    rows, cols, channels = field.shape
    lat, lon = lax.axis_size("lat"), lax.axis_size("lon")
    nlon = cols * lon
    slots, nlat, degrees = legendre.shape
    pairs = rows // 2
    lat_pos, lon_pos = lax.axis_index("lat"), lax.axis_index("lon")

    slabs = lax.all_to_all(pack(field), "lon", split_axis=0, concat_axis=0, tiled=True)

    owned = order_slots.reshape(lat, 1, slots)
    row_orders = jnp.broadcast_to(owned, (lat, 2, slots)).reshape(-1)
    row_parts = jnp.broadcast_to(
        jnp.arange(2, dtype=jnp.int32)[None, :, None], (lat, 2, slots)
    ).reshape(-1)
    row_factor = jnp.where(row_orders == 0, 1.0, 2.0).astype(F32)
    columns = jnp.arange(nlon, dtype=jnp.int32)
    analysis_table = wave(columns[None, :], row_orders[:, None], row_parts[:, None], nlon).astype(BF16)
    own_columns = lon_pos * cols + jnp.arange(cols, dtype=jnp.int32)
    quarter_back = jnp.arange(2, dtype=jnp.int32)[:, None, None] * 3
    synthesis_table = (
        row_factor
        * wave(
            own_columns[None, :, None],
            row_orders[None, None, :],
            row_parts[None, None, :] + quarter_back,
            nlon,
        )
    ).astype(BF16)

    lane_weight = jnp.repeat(quad_weight * (1.0 / nlon), HALF)[None, :]
    spectrum = analysis(analysis_table, slabs.reshape(nlon, rows * HALF), lane_weight)
    spectrum = lax.all_to_all(
        spectrum.reshape(lat, -1, LANES), "lat", split_axis=0, concat_axis=0, tiled=True
    ).reshape(spectrum.shape)

    own_orders = lax.dynamic_slice_in_dim(order_slots, lat_pos * slots, slots)
    mask = (jnp.arange(degrees, dtype=jnp.int32)[None, :] >= own_orders[:, None]).astype(F32)
    filtered = legendre_round_trip(legendre, mask[:, None, :], spectrum, pairs)
    filtered = lax.all_to_all(
        filtered.reshape(lat, -1, LANES), "lat", split_axis=0, concat_axis=0, tiled=True
    ).reshape(filtered.shape)
    everywhere = lax.all_gather(regroup(filtered, pairs), "lon")

    responses = disco_responses(field, support_blocks, filter_values)
    weights = jnp.concatenate(
        [
            jnp.stack([spectral_weight[0], -spectral_weight[1]]).reshape(-1, channels),
            disco_weight.reshape(-1, channels),
        ]
    )
    output, terms = finish(everywhere, synthesis_table, responses, field, cotangent, weights)
    sums = sum_everywhere(terms).reshape(5, channels, channels)
    grad_spectral = jnp.stack([sums[0], -sums[1]])
    return (output, grad_spectral, sums[2:])


def solution(mesh):
    placed = (
        P("lat", "lon", None),
        P("lat", "lon", None),
        P("lat", None, None),
        P("lat"),
        P(),
        P("lat", None),
        P(None, "lat", None, None),
        P(),
        P(),
    )
    return jax.shard_map(
        local,
        mesh=mesh,
        in_specs=placed,
        out_specs=(P("lat", "lon", None), P(), P()),
        check_vma=False,
    )
```

time: 664 us -> 251 us (0.38); the launches traced: 653 us -> 249 us
  waiting for transfers between devices: 340 us -> 66.5 us
  local copies, waits for them, and re-layouts: 142 us -> 11.1 us
  blocking collectives: 22.4 us -> 65.6 us
  matrix products: 42.4 us -> 3.05 us
  Pallas kernels: 0 us -> 36.2 us
  starting transfers between devices: 62.6 us -> 34.1 us
  other arithmetic: 28.3 us -> 18.1 us
    psum x1 -> x0, waiting for transfers between devices: 254 us -> none  [local(): grad_spectral = lax.psum(jnp.stack([g_real, g_imag]), ('lat', 'lon'))]
    unnamed x61 -> x23, local copies, waits for them, and re-layouts: 55.9 us -> 6.17 us
    convert_element_type x14 -> x0, local copies, waits for them, and re-layouts: 45.7 us -> none  [the longest x4 11.5 us: legendre_forward(): shaped = spectrum.reshape(lat_rows, 2, mmax, -1).astype(bf16)]
    all_to_all x8 -> x3, waiting for transfers between devices: 85.6 us -> 47.5 us  [the longest x1 22 us: local(): lax.all_to_all(spectrum.reshape(lat, -1, LANES), 'lat', split_axis=0, con...]
    pallas_call x0 -> x5, Pallas kernels: none -> 36.2 us  [the longest x1 17.5 us: finish(): kernel_call(finish_kernel, (pairs,), [pl.BlockSpec((parts, 1, coefs, LANE...]
    all_to_all x1 -> x3, blocking collectives: 22.4 us -> 54.9 us  [the longest x1 24.6 us: sum_everywhere(): pieces = lax.all_to_all(padded, 'lat', 0, 0, tiled=True)]
    dot_general x21 -> x4, matrix products: 32.6 us -> 3.05 us  [the longest x3 2.92 us: disco_responses(): jnp.einsum('ab,boc->aoc', operator[tap], rimmed[:, tap:tap + cols], prefe...]
    all_to_all x11 -> x0, local copies, waits for them, and re-layouts: 28.8 us -> none  [the longest x4 14.2 us: longitude_transform(): lax.all_to_all(values, 'lon', split_axis=2, concat_axis=1, tiled=True)]
  transfers between devices with their start and end apart: 13 -> 8, of which waited for: 8 -> 5; matrix products, arithmetic and copies ran while one was open for 14% -> 10% of each run, Pallas kernels for 0% -> 1%
where the time goes in v1:
time: 251 us; the launch traced here: 249 us
  waiting for transfers between devices  66.5 us (26%)
  blocking collectives  65.6 us (26%)
  Pallas kernels  36.2 us (14%)
  starting transfers between devices  34.1 us (14%)
  other arithmetic  18.1 us (7%)
  between operations  14.4 us (6%)
  local copies, waits for them, and re-layouts  11.1 us (4%)
  matrix products  3.05 us (1%)
    all_to_all x1, blocking collectives, sum_everywhere(): pieces = lax.all_to_all(padded, 'lat', 0, 0, tiled=True)  24.6 us
    all_to_all x1, waiting for transfers between devices, local(): lax.all_to_all(spectrum.reshape(lat, -1, LANES), 'lat', split_axis=0, con...  22 us
    all_gather x1, waiting for transfers between devices, local(): everywhere = lax.all_gather(regroup(filtered, pairs), 'lon')  18.5 us
    all_to_all x1, blocking collectives, sum_everywhere(): lax.all_to_all(jnp.broadcast_to(own[None], (lat, step, channels)), 'lat',...  17.7 us
    pallas_call x1, Pallas kernels, finish(): kernel_call(finish_kernel, (pairs,), [pl.BlockSpec((parts, 1, coefs, LANE...  17.5 us
    all_to_all x1, waiting for transfers between devices, local(): lax.all_to_all(filtered.reshape(lat, -1, LANES), 'lat', split_axis=0, con...  16.9 us
    all_to_all x1, starting transfers between devices, local(): lax.all_to_all(spectrum.reshape(lat, -1, LANES), 'lat', split_axis=0, con...  14.5 us
    all_to_all x1, blocking collectives, sum_everywhere(): lax.all_to_all(terms.astype(BF16).reshape(lon, share, channels), 'lon', 0...  12.7 us
  transfers between devices with their start and end apart: 8, of which 5 were waited for; matrix products, arithmetic and copies ran while one was open for 10% of the time, Pallas kernels for 1%

profile of v1, /device:TPU:1, one launch (start us, length us, event | category | flops | bytes accessed | tf_op | source)
XLA Modules:
  0.0 249.0 jit_solution(11362427699377425991)
XLA Ops:
  7.2 3.8 %shard_map.112 = bf16[4,360,512]{2,1,0:T(8,128)(2,1)} custom-call(bf16[8,360,256]{2,1,0:T(8,128)(2,1)} %field_ref.3), custom_call_target="tpu_custom_call" | custom-call | bytes 4423680 | tf_op jit(solution)/shard_map/pallas_call | solution.py:62
  11.0 5.0 %all-to-all-start = ((bf16[4,360,512]{2,1,0:T(8,128)(2,1)}), bf16[4,360,512]{2,1,0:T(8,128)(2,1)S(1)}, u32[]{:S(2)}, u32[]{:S(2)}) async-start(bf16[4,360,512]{2,1,0:T(8,128)(2,1)} %shard_map.112), calls=%async_computation | async-start | bytes 2949120 | tf_op jit(solution)/shard_map/all_to_all | solution.py:331
  17.2 7.9 %fusion.2.table_ref = bf16[768,1440]{1,0:T(8,128)(2,1)} fusion(f32[768]{0:T(1024)S(1)} %convert_element_type.81, s32[768]{0:T(1024)S(1)} %mul.175), kind=kLoop, calls=%fused_computation.4 | loop fusion | flops 39813120 | bytes 2217984 | tf_op jit(solution)/shard_map/convert_element_type | solution.py:340
  25.1 8.7 %all-to-all-done = bf16[4,360,512]{2,1,0:T(8,128)(2,1)S(1)} async-done(((bf16[4,360,512]{2,1,0:T(8,128)(2,1)}), bf16[4,360,512]{2,1,0:T(8,128)(2,1)S(1)}, u32[]{:S(2)}, u32[]{:S(2)}) %all-to-all-start) | async-done | bytes 1474592 | tf_op jit(solution)/shard_map/all_to_all | solution.py:331
  33.8 1.1 copy-done.2
  34.9 5.0 %shard_map.113 = bf16[3072,128]{1,0:T(8,128)(2,1)} custom-call(bf16[768,1440]{1,0:T(8,128)(2,1)} %fusion.2.table_ref, bf16[1440,512]{1,0:T(8,128)(2,1)} %bitcast.40, f32[1,512]{1,0:T(1,128)} %broadcast_in_dim_reshape.12.weight_ref), custom_call_target="tpu_custom_call" | custom-call | flops 1132462080 | bytes 2359296 | tf_op jit(solution)/shard_map/pallas_call | solution.py:88
  39.9 14.5 %all-to-all-start.1 = ((bf16[64,48,128]{2,1,0:T(8,128)(2,1)}), bf16[64,48,128]{2,1,0:T(8,128)(2,1)S(1)}, u32[]{:S(2)}, u32[]{:S(2)}) async-start(bf16[64,48,128]{2,1,0:T(8,128)(2,1)} %bitcast.47), calls=%async_computation.1 | async-start | bytes 1572864 | tf_op jit(solution)/shard_map/all_to_all | solution.py:355
  55.2 22.0 %all-to-all-done.1 = bf16[64,48,128]{2,1,0:T(8,128)(2,1)S(1)} async-done(((bf16[64,48,128]{2,1,0:T(8,128)(2,1)}), bf16[64,48,128]{2,1,0:T(8,128)(2,1)S(1)}, u32[]{:S(2)}, u32[]{:S(2)}) %all-to-all-start.1) | async-done | bytes 786464 | tf_op jit(solution)/shard_map/all_to_all | solution.py:355
  78.0 7.5 %shard_map.114 = bf16[3072,128]{1,0:T(8,128)(2,1)} custom-call(bf16[6,512,384]{2,1,0:T(8,128)(2,1)} %leg_ref.1, f32[6,1,384]{2,1,0:T(1,128)} %compare_convert_fusion.mask_ref, bf16[3072,128]{1,0:T(8,128)(2,1)} %bitcast.45), custom_call_target="tpu_custom_call" | custom-call | flops 603979776 | bytes 2359296 | tf_op jit(solution)/shard_map/pallas_call | solution.py:146
  85.6 6.2 %all-to-all-start.2 = ((bf16[64,48,128]{2,1,0:T(8,128)(2,1)}), bf16[64,48,128]{2,1,0:T(8,128)(2,1)S(1)}, u32[]{:S(2)}, u32[]{:S(2)}) async-start(bf16[64,48,128]{2,1,0:T(8,128)(2,1)} %bitcast.46), calls=%async_computation.2 | async-start | bytes 1572864 | tf_op jit(solution)/shard_map/all_to_all | solution.py:362
  91.9 1.4 copy.34
  93.3 3.7 %collective-permute-start = (bf16[8,360,256]{2,0,1:T(8,128)(2,1)}, bf16[8,360,256]{2,0,1:T(8,128)(2,1)}, u32[]{:S(2)}, u32[]{:S(2)}) collective-permute-start(bf16[8,360,256]{2,0,1:T(8,128)(2,1)} %copy.34), channel_id=1, source_target_pairs={{0,4},{4,8},{8,12},{12,16},{16,20},{20,24},{24,28},{28,32},{32,36}... | collective-permute-start | bytes 4423688 | tf_op jit(solution)/shard_map/ppermute | solution.py:268
  97.0 1.9 collective-permute-start.1
  98.9 16.9 %all-to-all-done.2 = bf16[64,48,128]{2,1,0:T(8,128)(2,1)S(1)} async-done(((bf16[64,48,128]{2,1,0:T(8,128)(2,1)}), bf16[64,48,128]{2,1,0:T(8,128)(2,1)S(1)}, u32[]{:S(2)}, u32[]{:S(2)}) %all-to-all-start.2) | async-done | bytes 786464 | tf_op jit(solution)/shard_map/all_to_all | solution.py:362
  116.7 2.3 shard_map.115
  119.3 0.9 pad_maximum_fusion.5.weight_ref
  120.9 3.3 %fusion.13.table_ref = bf16[2,360,768]{2,1,0:T(8,128)(2,1)} fusion(f32[360,768]{1,0:T(8,128)S(1)} %get-tuple-element.18, f32[360,768]{1,0:T(8,128)S(1)} %get-tuple-element.17, f32[2,768]{1,0:T(2,128)S(1)} %add_convert_fusion, f32[360,768]{1,0:T(8,128)S(1)} %get-tuple-element.16, f32[768]{0:T(1024)S(1)} %compare_select_fusion), kind=kLoop, calls=%fused_computation.27 | loop fusion | flops 16035840 | bytes 4432896 | tf_op jit(solution)/shard_map/convert_element_type | solution.py:351
  124.2 1.6 constant_dynamic-update-slice_fusion.2
  126.0 1.5 constant_dynamic-update-slice_fusion
  127.9 2.4 collective-permute-start.3
  130.3 1.0 fusion.30
  132.0 1.0 fusion.5
  133.3 1.0 fusion.3
  134.6 2.4 pad_maximum_fusion.4.resp_ref
  137.0 18.5 %all-gather.3.cloned.1.call-done = bf16[16,768,128]{2,1,0:T(8,128)(2,1)} async-done(((bf16[4,768,128]{2,1,0:T(8,128)(2,1)}), bf16[16,768,128]{2,1,0:T(8,128)(2,1)}) %all-gather.3.cloned.1.call-update) | async-done | bytes 3145744 | tf_op jit(solution)/shard_map/all_gather | solution.py:365
  155.5 17.5 %shard_map.116 = (bf16[8,360,256]{2,1,0:T(8,128)(2,1)}, f32[1280,256]{1,0:T(8,128)}) custom-call(bf16[4,4,768,128]{3,2,1,0:T(8,128)(2,1)} %bitcast.52, bf16[2,360,768]{2,1,0:T(8,128)(2,1)} %fusion.13.table_ref, bf16[3,8,360,256]{3,2,1,0:T(8,128)(2,1)} %pad_maximum_fusion.4.resp_ref, bf16[8,360,256]{2,1,0:T(8,128)(2,1)} %field_ref.3, ...), custom_call_target="tpu_custom_call" | custom-call | flops 6039797760 | bytes 8355840 | tf_op jit(solution)/shard_map/pallas_call | solution.py:225
  173.0 1.4 convert_element_type.91
  174.4 12.7 %all_to_all.30 = bf16[4,320,256]{2,1,0:T(8,128)(2,1)S(1)} all-to-all(bf16[4,320,256]{2,1,0:T(8,128)(2,1)S(1)} %bitcast.48), channel_id=1, replica_groups=mesh['lat'=64,'lon'=4] {'lon'}, dimensions={0} | all-to-all | bytes 1310720 | tf_op jit(solution)/shard_map/all_to_all | solution.py:297
  187.2 24.6 %all_to_all.31 = bf16[64,8,256]{2,1,0:T(8,128)(2,1)S(1)} all-to-all(bf16[64,8,256]{2,1,0:T(8,128)(2,1)S(1)} %pad_bitcast_fusion), channel_id=1, replica_groups=mesh['lat'=64,'lon'=4] {'lat'}, dimensions={0} | all-to-all | bytes 524288 | tf_op jit(solution)/shard_map/all_to_all | solution.py:303
  211.9 17.7 %all_to_all.32 = bf16[64,8,256]{2,1,0:T(8,128)(2,1)S(1)} all-to-all(bf16[64,8,256]{2,1,0:T(8,128)(2,1)S(1)} %broadcast_in_dim.73), channel_id=1, replica_groups=mesh['lat'=64,'lon'=4] {'lat'}, dimensions={0} | all-to-all | bytes 524288 | tf_op jit(solution)/shard_map/all_to_all | solution.py:305
  229.5 10.7 %all_gather.11 = bf16[1280,256]{1,0:T(8,128)(2,1)S(1)} all-gather(bf16[320,256]{1,0:T(8,128)(2,1)S(1)} %slice_bitcast_fusion.1), channel_id=1, replica_groups=mesh['lat'=64,'lon'=4] {'lon'}, dimensions={0}, use_global_device_ids=true | all-gather | bytes 819200 | tf_op jit(solution)/shard_map/all_gather | solution.py:309
  240.3 0.9 slice.78
  (63 shorter events, 7.8 us)
Async XLA Ops:
  7.2 112.0 %copy-start = (bf16[3,8,3,8]{3,1,2,0:T(8,128)(2,1)S(1)}, bf16[3,8,3,8]{3,1,2,0:T(8,128)(2,1)}, u32[]{:S(2)}) copy-start(bf16[3,8,3,8]{3,1,2,0:T(8,128)(2,1)} %param.15) | copy-start | bytes 3460
  7.2 8.8 %copy-start.7 = (s32[384]{0:T(512)S(1)}, s32[384]{0:T(512)}, u32[]{:S(2)}) copy-start(s32[384]{0:T(512)} %param.13) | copy-start | bytes 4612
  11.0 5.5 %copy-start.8 = (f32[8]{0:T(128)S(1)}, f32[8]{0:T(128)}, u32[]{:S(2)}) copy-start(f32[8]{0:T(128)} %param.12) | copy-start | bytes 100
  11.0 22.7 %all-to-all-start = ((bf16[4,360,512]{2,1,0:T(8,128)(2,1)}), bf16[4,360,512]{2,1,0:T(8,128)(2,1)S(1)}, u32[]{:S(2)}, u32[]{:S(2)}) async-start(bf16[4,360,512]{2,1,0:T(8,128)(2,1)} %shard_map.112), calls=%async_computation | async-start | bytes 2949120 | tf_op jit(solution)/shard_map/all_to_all | solution.py:331
  33.8 1.1 copy-start.2
  39.9 37.3 %all-to-all-start.1 = ((bf16[64,48,128]{2,1,0:T(8,128)(2,1)}), bf16[64,48,128]{2,1,0:T(8,128)(2,1)S(1)}, u32[]{:S(2)}, u32[]{:S(2)}) async-start(bf16[64,48,128]{2,1,0:T(8,128)(2,1)} %bitcast.47), calls=%async_computation.1 | async-start | bytes 1572864 | tf_op jit(solution)/shard_map/all_to_all | solution.py:355
  77.2 0.9 copy-start.4
  78.0 13.8 %copy-start.1 = (bf16[8,360,256]{2,1,0:T(8,128)(2,1)S(1)}, bf16[8,360,256]{2,1,0:T(8,128)(2,1)}, u32[]{:S(2)}) copy-start(bf16[8,360,256]{2,1,0:T(8,128)(2,1)} %field_ref.3) | copy-start | bytes 4423684
  85.6 30.2 %all-to-all-start.2 = ((bf16[64,48,128]{2,1,0:T(8,128)(2,1)}), bf16[64,48,128]{2,1,0:T(8,128)(2,1)S(1)}, u32[]{:S(2)}, u32[]{:S(2)}) async-start(bf16[64,48,128]{2,1,0:T(8,128)(2,1)} %bitcast.46), calls=%async_computation.2 | async-start | bytes 1572864 | tf_op jit(solution)/shard_map/all_to_all | solution.py:362
  91.8 27.2 %copy-start.6 = (bf16[2,256,256]{2,1,0:T(8,128)(2,1)S(1)}, bf16[2,256,256]{2,1,0:T(8,128)(2,1)}, u32[]{:S(2)}) copy-start(bf16[2,256,256]{2,1,0:T(8,128)(2,1)} %param.16) | copy-start | bytes 786436
  91.8 63.6 %all-gather.3.cloned.1.call-start = ((), (), s32[]{:S(2)}) async-start(), calls=%async_computation.6 | async-start | bytes 3932160 | tf_op jit(solution)/shard_map/all_gather | solution.py:365
  93.3 25.8 %copy-start.9 = (s32[1,3]{1,0:T(1,128)S(1)}, s32[1,3]{1,0:T(1,128)}, u32[]{:S(2)}) copy-start(s32[1,3]{1,0:T(1,128)} %param.14) | copy-start | bytes 40
  93.3 26.0 %copy-start.5 = (bf16[3,256,256]{2,1,0:T(8,128)(2,1)S(1)}, bf16[3,256,256]{2,1,0:T(8,128)(2,1)}, u32[]{:S(2)}) copy-start(bf16[3,256,256]{2,1,0:T(8,128)(2,1)} %param.17) | copy-start | bytes 1179652
  93.3 30.9 %collective-permute-start = (bf16[8,360,256]{2,0,1:T(8,128)(2,1)}, bf16[8,360,256]{2,0,1:T(8,128)(2,1)}, u32[]{:S(2)}, u32[]{:S(2)}) collective-permute-start(bf16[8,360,256]{2,0,1:T(8,128)(2,1)} %copy.34), channel_id=1, source_target_pairs={{0,4},{4,8},{8,12},{12,16},{16,20},{20,24},{24,28},{28,32},{32,36}... | collective-permute-start | bytes 4423688 | tf_op jit(solution)/shard_map/ppermute | solution.py:268
  97.0 29.1 %collective-permute-start.1 = (bf16[8,360,256]{2,0,1:T(8,128)(2,1)}, bf16[8,360,256]{2,0,1:T(8,128)(2,1)}, u32[]{:S(2)}, u32[]{:S(2)}) collective-permute-start(bf16[8,360,256]{2,0,1:T(8,128)(2,1)} %copy.34), channel_id=1, source_target_pairs={{4,0},{8,4},{12,8},{16,12},{20,16},{24,20},{28,24},{32,28},{36,32}... | collective-permute-start | bytes 4423688 | tf_op jit(solution)/shard_map/ppermute | solution.py:268
  115.8 0.9 copy-start.3
  127.6 4.4 %collective-permute-start.2 = (bf16[24,1,256]{2,0,1:T(8,128)(2,1)S(1)}, bf16[24,1,256]{2,0,1:T(8,128)(2,1)S(1)}, u32[]{:S(2)}, u32[]{:S(2)}) collective-permute-start(bf16[24,1,256]{2,0,1:T(8,128)(2,1)S(1)} %get-tuple-element.7), channel_id=1, source_target_pairs={{0,1},{1,2},{2,3},{3,0},{4,5},{5,6},{6,7},{7,4},{8,9},{9,10},{10,1... | collective-permute-start | bytes 36872 | tf_op jit(solution)/shard_map/ppermute | solution.py:273
  127.9 5.4 %collective-permute-start.3 = (bf16[24,1,256]{2,0,1:T(8,128)(2,1)S(1)}, bf16[24,1,256]{2,0,1:T(8,128)(2,1)S(1)}, u32[]{:S(2)}, u32[]{:S(2)}) collective-permute-start(bf16[24,1,256]{2,0,1:T(8,128)(2,1)S(1)} %get-tuple-element.8), channel_id=1, source_target_pairs={{1,0},{2,1},{3,2},{0,3},{5,4},{6,5},{7,6},{4,7},{9,8},{10,9},{11,1... | collective-permute-start | bytes 36872 | tf_op jit(solution)/shard_map/ppermute | solution.py:274
Sparse Core Ops, SparseCore 0:
  119.1 36.2 all-gather.2

commit v2 on v0

v2 whole, which is shorter than its diff:
```python
import functools
import math

import jax
import jax.numpy as jnp
from jax import lax
from jax.experimental import pallas as pl
from jax.experimental.pallas import tpu as pltpu
from jax.sharding import PartitionSpec as P

F32 = jnp.float32
BF16 = jnp.bfloat16
LANES = 128
HALF = LANES // 2
GELU_SCALE = math.sqrt(2.0 / math.pi)
GELU_CUBE = 0.044715


def vmem_call(kernel, operands, out_shape, scratch=(), limit=32, far=()):
    place = pl.BlockSpec(memory_space=pltpu.VMEM)
    places = [pl.BlockSpec(memory_space=pltpu.HBM) if i in far else place for i in range(len(operands))]
    return pl.pallas_call(
        kernel,
        in_specs=places,
        out_specs=jax.tree.map(lambda _: place, out_shape),
        out_shape=out_shape,
        scratch_shapes=list(scratch),
        compiler_params=pltpu.CompilerParams(vmem_limit_bytes=limit << 20),
        cost_estimate=pl.CostEstimate(flops=0, bytes_accessed=1 << 20, transcendentals=0),
    )(*operands)


def low_lanes(rows):
    return lax.broadcasted_iota(jnp.int32, (rows, LANES), 1) < HALF


def swap(value):
    return pltpu.roll(value, HALF, 1)


def exchange(low, first, second):
    return (jnp.where(low, first, swap(second)), jnp.where(low, swap(first), second))


def copy_kernel(value_ref, after_ref, out_ref):
    out_ref[...] = value_ref[...]


def copy_behind(value, after):
    shape = jax.ShapeDtypeStruct(value.shape, value.dtype)
    return vmem_call(copy_kernel, [value, after], shape, far=(1,))


def pack_kernel(field_ref, *out_refs):
    rows, cols, _ = field_ref.shape
    parts = len(out_refs)
    low = low_lanes(cols)
    for ahead, out_ref in enumerate(out_refs):
        quarter = lax.rem(lax.axis_index("lon") + ahead, parts)
        upper = lax.rem(quarter, 2)
        lanes = pl.ds(pl.multiple_of((quarter // 2) * LANES, LANES), LANES)
        for pair in range(rows // 2):
            first = pltpu.roll(field_ref[2 * pair, :, lanes].astype(F32), upper * HALF, 1)
            second = pltpu.roll(field_ref[2 * pair + 1, :, lanes].astype(F32), HALF - upper * HALF, 1)
            out_ref[:, pair * LANES : (pair + 1) * LANES] = jnp.where(low, first, second).astype(BF16)


def pack(field):
    rows, cols, channels = field.shape
    parts = channels // HALF
    return vmem_call(
        pack_kernel, [field], [jax.ShapeDtypeStruct((cols, rows * HALF), BF16)] * parts
    )


def quarter_wave(units, nlon):
    angle = units * (2.0 * math.pi / nlon)
    square = angle * angle
    total = jnp.full_like(square, 1.0 / math.factorial(12))
    for power in (10, 8, 6, 4, 2, 0):
        total = total * square + (-1.0) ** (power // 2) / math.factorial(power)
    return total


def whole_mod_four(value):
    return value - 4.0 * jnp.floor(value * 0.25)


def wave(column, order, ahead, nlon):
    quarter = nlon // 4
    phase = column * order
    turns = jnp.floor((phase + 0.5) * (1.0 / quarter))
    rest = phase - turns * quarter
    cosine = quarter_wave(rest, nlon)
    sine = quarter_wave(quarter - rest, nlon)
    turns = whole_mod_four(turns + ahead)
    odd = (turns == 1.0) | (turns == 3.0)
    here = jnp.where(odd, sine, cosine)
    further = jnp.where(odd, cosine, sine)
    here = jnp.where((turns == 1.0) | (turns == 2.0), -here, here)
    further = jnp.where(turns < 1.5, -further, further)
    return (here, further)


def advance(here, further, turns):
    turns = whole_mod_four(turns)
    even = (turns == 0.0).astype(F32) - (turns == 2.0).astype(F32)
    odd = (turns == 1.0).astype(F32) - (turns == 3.0).astype(F32)
    return even * here + odd * further


def table_kernel(down_ref, across_ref, after_ref, analysis_ref, synthesis_ref):
    parts, rows, cols = analysis_ref.shape
    nlon = parts * cols
    place = lax.axis_index("lon")
    order, part = down_ref[:, 0:1], down_ref[:, 1:2]
    column = lax.broadcasted_iota(jnp.int32, (rows, cols), 1).astype(F32)
    here, further = wave(column, order, part, nlon)
    for k in range(parts):
        slab = lax.rem(place + parts - k, parts).astype(F32)
        analysis_ref[k] = advance(here, further, slab * order).astype(BF16)
    order, part = across_ref[0:1, :], across_ref[1:2, :]
    column = lax.broadcasted_iota(jnp.int32, (cols, rows), 0).astype(F32)
    here, further = wave(column, order, part, nlon)
    factor = jnp.where(order == 0.0, 1.0, 2.0)
    turns = place.astype(F32) * order
    for back in range(2):
        synthesis_ref[back] = (factor * advance(here, further, turns + back)).astype(BF16)


def fourier_tables(row_orders, row_parts, parts, after):
    coefs, cols = row_orders.shape[0], after.shape[1]
    both = jnp.stack([row_orders, row_parts]).astype(F32)
    return vmem_call(
        table_kernel,
        [both.T, both, after],
        [
            jax.ShapeDtypeStruct((parts, coefs, cols), BF16),
            jax.ShapeDtypeStruct((2, cols, coefs), BF16),
        ],
        far=(2,),
    )


def analysis_kernel(parts, table_ref, *refs):
    weight_ref, out_ref, wide_ref = refs[parts:]
    rows = table_ref.shape[1]
    total = jnp.dot(table_ref[0], refs[0][...], preferred_element_type=F32)
    for k in range(1, parts):
        total += jnp.dot(table_ref[k], refs[k][...], preferred_element_type=F32)
    total = total * weight_ref[...]
    pairs = total.shape[1] // LANES
    for pair in range(pairs):
        wide_ref[pl.ds(pair, rows, stride=pairs), :] = total[:, pair * LANES : (pair + 1) * LANES]
    out_ref[...] = wide_ref[...].astype(BF16)


def analysis(table, pieces, weight):
    parts, coefs, _ = table.shape
    shape = (coefs * weight.shape[1] // LANES, LANES)
    return vmem_call(
        functools.partial(analysis_kernel, parts),
        [table, *pieces, weight],
        jax.ShapeDtypeStruct(shape, BF16),
        [pltpu.VMEM(shape, F32)],
    )


def legendre_kernel(pairs, far_ref, mask_ref, spec_ref, out_ref, leg_ref, wide_ref, lat_ref, back_ref, sems):
    slots, nlat, _ = leg_ref.shape
    loads = [pltpu.make_async_copy(far_ref.at[k], leg_ref.at[k], sems.at[k]) for k in range(slots)]
    for load in loads:
        load.start()
    rows = 2 * pairs
    blocks = nlat // rows
    piece = 2 * slots * pairs
    low = low_lanes(blocks)
    wide_ref[...] = spec_ref[...].astype(F32)
    for slot in range(slots):
        lat = lat_ref.at[slot]

        def taken(part, pair):
            return pl.ds((part * slots + slot) * pairs + pair, blocks, stride=piece)

        for pair in range(pairs):
            even, odd = exchange(low, wide_ref[taken(0, pair), :], wide_ref[taken(1, pair), :])
            lat[pl.ds(2 * pair, blocks, stride=rows), :] = even
            lat[pl.ds(2 * pair + 1, blocks, stride=rows), :] = odd
        loads[slot].wait()
        leg = leg_ref[slot]
        coeffs = lax.dot_general(
            lat[...].astype(BF16), leg, (((0,), (0,)), ((), ())), preferred_element_type=F32
        )
        coeffs = (coeffs * mask_ref[slot]).astype(BF16)
        lat[...] = lax.dot_general(leg, coeffs, (((1,), (1,)), ((), ())), preferred_element_type=F32)
        for pair in range(pairs):
            real, imag = exchange(
                low,
                lat[pl.ds(2 * pair, blocks, stride=rows), :],
                lat[pl.ds(2 * pair + 1, blocks, stride=rows), :],
            )
            back_ref[taken(0, pair), :] = real
            back_ref[taken(1, pair), :] = imag
    out_ref[...] = back_ref[...].astype(BF16)


def legendre_round_trip(legendre, mask, spectrum, pairs):
    slots, nlat, _ = legendre.shape
    return vmem_call(
        functools.partial(legendre_kernel, pairs),
        [legendre, mask, spectrum],
        jax.ShapeDtypeStruct(spectrum.shape, BF16),
        [
            pltpu.VMEM(legendre.shape, BF16),
            pltpu.VMEM(spectrum.shape, F32),
            pltpu.VMEM((slots, nlat, LANES), F32),
            pltpu.VMEM(spectrum.shape, F32),
            pltpu.SemaphoreType.DMA((slots,)),
        ],
        far=(0,),
    )


def finish_kernel(
    own_ref,
    west_ref,
    far_west_ref,
    far_east_ref,
    east_ref,
    table_ref,
    resp_ref,
    disco_ref,
    field_ref,
    cot_ref,
    weight_ref,
    out_ref,
    grad_ref,
    wide_ref,
    mix_ref,
    total_ref,
):
    pairs, _, channels = field_ref.shape
    parts, rows, _ = wide_ref.shape
    coefs = rows // pairs
    low = low_lanes(coefs)
    place = lax.axis_index("lon")
    wide_ref[place] = own_ref[...].astype(F32)
    wide_ref[lax.rem(place + parts - 1, parts)] = west_ref[...].astype(F32)
    wide_ref[lax.rem(place + 1, parts)] = east_ref[...].astype(F32)
    across = lax.rem(place + 2, parts)
    middle = rows // 2
    wide_ref[across, :middle] = far_west_ref[...].astype(F32)
    wide_ref[across, middle:] = far_east_ref[...].astype(F32)
    for pair in range(pairs):
        mix = mix_ref.at[pair]
        held = [wide_ref[part, pl.ds(pair, coefs, stride=pairs), :] for part in range(parts)]
        tiles = [exchange(low, held[2 * i], held[2 * i + 1]) for i in range(parts // 2)]
        spectrum = jnp.concatenate([tile[half] for half in range(2) for tile in tiles], axis=1)
        spectrum = spectrum.astype(BF16)
        for part in range(2):
            grid = jnp.dot(table_ref[part], spectrum, preferred_element_type=F32)
            grid = jnp.concatenate([grid[:, :channels], grid[:, channels:]], axis=0)
            mix[:, part * channels : (part + 1) * channels] = grid.astype(BF16)
        pre = jnp.dot(mix[...], weight_ref[...], preferred_element_type=F32) + disco_ref[pair]
        square = pre * pre
        bend = jnp.tanh(GELU_SCALE * (pre + GELU_CUBE * (square * pre)))
        activated = 0.5 * pre * (1.0 + bend)
        slope = 0.5 * (1.0 + bend) + 0.5 * pre * (1.0 - bend * bend) * (
            GELU_SCALE * (1.0 + 3.0 * GELU_CUBE * square)
        )
        out_ref[pair] = (field_ref[pair].astype(F32) + activated).astype(BF16)
        grad_pre = (cot_ref[pair].astype(F32) * slope).astype(BF16)
        start = 0
        for values in [mix[...]] + [resp_ref[tap, pair] for tap in range(resp_ref.shape[0])]:
            term = lax.dot_general(
                grad_pre, values, (((0,), (0,)), ((), ())), preferred_element_type=F32
            )
            span = slice(start, start + values.shape[1])
            start = span.stop
            if pair == 0:
                total_ref[:, span] = term
            else:
                total_ref[:, span] += term
    for part in range(grad_ref.shape[0] // channels):
        span = slice(part * channels, (part + 1) * channels)
        grad_ref[span, :] = total_ref[:, span].T.astype(BF16)


def finish(spectra, table, responses, disco_sum, field, cotangent, weight):
    rows, cols, channels = field.shape
    pairs = rows // 2
    grouped = (pairs, 2 * cols, channels)
    taps = responses.shape[0]
    stacked = weight.shape[0] + taps * channels
    output, grads = vmem_call(
        finish_kernel,
        [
            *spectra,
            table,
            responses.reshape(taps, *grouped),
            disco_sum.reshape(grouped),
            field.reshape(grouped),
            cotangent.reshape(grouped),
            weight,
        ],
        [jax.ShapeDtypeStruct(grouped, BF16), jax.ShapeDtypeStruct((stacked, channels), BF16)],
        [
            pltpu.VMEM((channels // HALF, spectra[0].shape[0], LANES), F32),
            pltpu.VMEM((pairs, 2 * cols, weight.shape[0]), BF16),
            pltpu.VMEM((channels, stacked), F32),
        ],
    )
    return output.reshape(field.shape), grads


def turn(value, axis, by):
    size = lax.axis_size(axis)
    return lax.ppermute(value, axis, [(i, (i + by) % size) for i in range(size)])


def halo(field):
    size = lax.axis_size("lat")
    up = [(i, i + 1) for i in range(size - 1)]
    down = [(j, i) for i, j in up]
    return (lax.ppermute(field, "lat", up), lax.ppermute(field, "lat", down))


def disco_responses(above, field, below, support_blocks, filter_values):
    rows, cols, _ = field.shape
    lat_pos = lax.axis_index("lat")
    blocks = jnp.concatenate([above, field, below], axis=0)
    picks = support_blocks[0] - lat_pos + 1
    onehot = (picks[:, None] == jnp.arange(3, dtype=jnp.int32)[None, :]).astype(F32)
    operator = (
        jnp.einsum("tasb,sq->taqb", filter_values.astype(F32), onehot)
        .reshape(3, rows, 3 * rows)
        .astype(BF16)
    )
    here, level, there = (
        jnp.einsum("ab,boc->aoc", operator[tap], blocks, preferred_element_type=F32).astype(BF16)
        for tap in range(3)
    )
    first = turn(here[:, cols - 1 :], "lon", 1)
    last = turn(there[:, :1], "lon", -1)
    return jnp.stack(
        [
            jnp.concatenate([first, here[:, : cols - 1]], axis=1),
            level,
            jnp.concatenate([there[:, 1:], last], axis=1),
        ]
    )


def sum_everywhere(terms):
    rows, channels = terms.shape
    lon, lat = lax.axis_size("lon"), lax.axis_size("lat")
    side = 8 if lat % 8 == 0 else lat
    count = side * lon
    planes = [list(range(z * count, (z + 1) * count)) for z in range(lat // side)]
    columns = [list(range(i, lat, side)) for i in range(side)]
    share = rows // count
    pieces = lax.all_to_all(
        terms.reshape(count, share, channels),
        ("lat", "lon"),
        0,
        0,
        tiled=True,
        axis_index_groups=planes,
    )
    own = jnp.sum(pieces.astype(F32), axis=0).astype(BF16)
    others = lax.all_to_all(
        jnp.broadcast_to(own[None], (lat // side, share, channels)),
        "lat",
        0,
        0,
        tiled=True,
        axis_index_groups=columns,
    )
    total = jnp.sum(others.astype(F32), axis=0).astype(BF16)
    everything = lax.all_to_all(
        jnp.broadcast_to(total[None], (count, share, channels)),
        ("lat", "lon"),
        0,
        0,
        tiled=True,
        axis_index_groups=planes,
    )
    return everything.reshape(rows, channels).astype(F32)


def local(
    field,
    cotangent,
    legendre,
    quad_weight,
    order_slots,
    support_blocks,
    filter_values,
    spectral_weight,
    disco_weight,
):
    rows, cols, channels = field.shape
    lat, lon = lax.axis_size("lat"), lax.axis_size("lon")
    nlon = cols * lon
    slots, nlat, degrees = legendre.shape
    pairs = rows // 2
    lat_pos, lon_pos = lax.axis_index("lat"), lax.axis_index("lon")

    pieces = pack(field)
    slabs = [pieces[0]] + [turn(pieces[k], "lon", k) for k in range(1, lon)]

    row_orders = jnp.broadcast_to(order_slots.reshape(lat, 1, slots), (lat, 2, slots)).reshape(-1)
    row_parts = jnp.broadcast_to(
        jnp.arange(2, dtype=jnp.int32)[None, :, None], (lat, 2, slots)
    ).reshape(-1)
    copied = copy_behind(field, pieces[0])
    above, below = halo(copied)
    analysis_table, synthesis_table = fourier_tables(row_orders, row_parts, lon, copied)
    lane_weight = jnp.repeat(quad_weight * (1.0 / nlon), HALF)[None, :]
    spectrum = analysis(analysis_table, slabs, lane_weight)
    own_orders = lax.dynamic_slice_in_dim(order_slots, lat_pos * slots, slots)
    mask = (jnp.arange(degrees, dtype=jnp.int32)[None, :] >= own_orders[:, None]).astype(F32)
    spectrum, above, below, mask = lax.optimization_barrier((spectrum, above, below, mask))
    spectrum = lax.all_to_all(
        spectrum.reshape(lat, -1, LANES), "lat", split_axis=0, concat_axis=0, tiled=True
    ).reshape(spectrum.shape)
    filtered = legendre_round_trip(legendre, mask[:, None, :], spectrum, pairs)
    filtered = lax.all_to_all(
        filtered.reshape(lat, -1, LANES), "lat", split_axis=0, concat_axis=0, tiled=True
    ).reshape(filtered.shape)
    filtered, above, below = lax.optimization_barrier((filtered, above, below))
    west, east = turn(filtered, "lon", 1), turn(filtered, "lon", -1)
    middle = filtered.shape[0] // 2
    far_west, far_east = turn(west[:middle], "lon", 1), turn(east[middle:], "lon", -1)
    responses = disco_responses(above, field, below, support_blocks, filter_values)
    disco_sum = sum(
        jnp.dot(responses[tap].reshape(-1, channels), disco_weight[tap], preferred_element_type=F32)
        for tap in range(responses.shape[0])
    )

    output, terms = finish(
        (filtered, west, far_west, far_east, east),
        synthesis_table,
        responses,
        disco_sum,
        field,
        cotangent,
        spectral_weight.reshape(-1, channels),
    )
    sums = sum_everywhere(terms)
    spectral = spectral_weight.shape[0] * channels
    return (
        output,
        sums[:spectral].reshape(spectral_weight.shape),
        sums[spectral:].reshape(disco_weight.shape),
    )


def solution(mesh):
    placed = (
        P("lat", "lon", None),
        P("lat", "lon", None),
        P("lat", None, None),
        P("lat"),
        P(),
        P("lat", None),
        P(None, "lat", None, None),
        P(),
        P(),
    )
    return jax.shard_map(
        local,
        mesh=mesh,
        in_specs=placed,
        out_specs=(P("lat", "lon", None), P(), P()),
        check_vma=False,
    )
```

time: 664 us -> 206 us (0.31); the launches traced: 653 us -> 202 us
  waiting for transfers between devices: 340 us -> 65.7 us
  local copies, waits for them, and re-layouts: 142 us -> 8.06 us
  matrix products: 42.4 us -> 5.72 us
  Pallas kernels: 0 us -> 28.9 us
  blocking collectives: 22.4 us -> 51.1 us
  other arithmetic: 28.3 us -> 3.35 us
  starting transfers between devices: 62.6 us -> 38.1 us
  between operations: 15 us -> 1.51 us
    psum x1 -> x0, waiting for transfers between devices: 254 us -> none  [local(): grad_spectral = lax.psum(jnp.stack([g_real, g_imag]), ('lat', 'lon'))]
    unnamed x61 -> x24, local copies, waits for them, and re-layouts: 55.9 us -> 3.09 us
    convert_element_type x14 -> x1, local copies, waits for them, and re-layouts: 45.7 us -> 0.3 us  [disco_responses(): jnp.einsum('ab,boc->aoc', operator[tap], blocks, preferred_element_type=F32)]
    all_to_all x8 -> x2, waiting for transfers between devices: 85.6 us -> 44.9 us  [the longest x1 22.6 us: local(): lax.all_to_all(spectrum.reshape(lat, -1, LANES), 'lat', split_axis=0, con...]
    all_to_all x8 -> x2, starting transfers between devices: 53.8 us -> 17.9 us  [the longest x1 11.6 us: local(): lax.all_to_all(spectrum.reshape(lat, -1, LANES), 'lat', split_axis=0, con...]
    pallas_call x0 -> x6, Pallas kernels: none -> 28.9 us  [vmem_call(): pl.pallas_call(kernel, in_specs=places, out_specs=jax.tree.map(lambda _:...]
    all_to_all x11 -> x0, local copies, waits for them, and re-layouts: 28.8 us -> none  [the longest x4 14.2 us: longitude_transform(): lax.all_to_all(values, 'lon', split_axis=2, concat_axis=1, tiled=True)]
    all_to_all x1 -> x3, blocking collectives: 22.4 us -> 51.1 us  [the longest x1 20.7 us: sum_everywhere(): lax.all_to_all(terms.reshape(count, share, channels), ('lat', 'lon'), 0,...]
  transfers between devices with their start and end apart: 13 -> 13, of which waited for: 8 -> 6; matrix products, arithmetic and copies ran while one was open for 14% -> 5% of each run, Pallas kernels for 0% -> 6%
where the time goes in v2:
time: 206 us; the launch traced here: 202 us
  waiting for transfers between devices  65.7 us (32%)
  blocking collectives  51.1 us (25%)
  starting transfers between devices  38.1 us (18%)
  Pallas kernels  28.9 us (14%)
  local copies, waits for them, and re-layouts  8.06 us (4%)
  matrix products  5.72 us (3%)
  other arithmetic  3.35 us (2%)
    pallas_call x6, Pallas kernels, vmem_call(): pl.pallas_call(kernel, in_specs=places, out_specs=jax.tree.map(lambda _:...  28.9 us
    all_to_all x1, waiting for transfers between devices, local(): lax.all_to_all(spectrum.reshape(lat, -1, LANES), 'lat', split_axis=0, con...  22.6 us
    all_to_all x1, waiting for transfers between devices, local(): lax.all_to_all(filtered.reshape(lat, -1, LANES), 'lat', split_axis=0, con...  22.3 us
    ppermute x9, waiting for transfers between devices, turn(): lax.ppermute(value, axis, [(i, (i + by) % size) for i in range(size)])  20.8 us
    all_to_all x1, blocking collectives, sum_everywhere(): lax.all_to_all(terms.reshape(count, share, channels), ('lat', 'lon'), 0,...  20.7 us
    all_to_all x1, blocking collectives, sum_everywhere(): lax.all_to_all(jnp.broadcast_to(total[None], (count, share, channels)), (...  18.5 us
    ppermute x9, starting transfers between devices, turn(): lax.ppermute(value, axis, [(i, (i + by) % size) for i in range(size)])  12.6 us
    all_to_all x1, blocking collectives, sum_everywhere(): lax.all_to_all(jnp.broadcast_to(own[None], (lat // side, share, channels)...  11.9 us
  transfers between devices with their start and end apart: 13, of which 6 were waited for; matrix products, arithmetic and copies ran while one was open for 5% of the time, Pallas kernels for 6%

profile of v2, /device:TPU:1, one launch (start us, length us, event | category | flops | bytes accessed | tf_op | source)
XLA Modules:
  0.0 202.4 jit_solution(10708873397776963283)
XLA Ops:
  0.7 1.4 copy-done.1
  2.0 1.6 shard_map.112
  3.7 4.6 %collective-permute-start.3 = (bf16[8,360,256]{2,1,0:T(8,128)(2,1)S(1)}, bf16[8,360,256]{2,1,0:T(8,128)(2,1)}, u32[]{:S(2)}, u32[]{:S(2)}) collective-permute-start(bf16[8,360,256]{2,1,0:T(8,128)(2,1)S(1)} %shard_map.113.after_ref), channel_id=1, source_target_pairs={{0,4},{4,8},{8,12},{12,16},{16,20},{20,24},{24,28},{28,32},{32,36}... | collective-permute-start | bytes 4423688 | tf_op jit(solution)/shard_map/ppermute | solution.py:325
  8.3 2.9 %collective-permute-start.4 = (bf16[8,360,256]{2,1,0:T(8,128)(2,1)S(1)}, bf16[8,360,256]{2,1,0:T(8,128)(2,1)}, u32[]{:S(2)}, u32[]{:S(2)}) collective-permute-start(bf16[8,360,256]{2,1,0:T(8,128)(2,1)S(1)} %shard_map.113.after_ref), channel_id=1, source_target_pairs={{4,0},{8,4},{12,8},{16,12},{20,16},{24,20},{28,24},{32,28},{36,32}... | collective-permute-start | bytes 4423688 | tf_op jit(solution)/shard_map/ppermute | solution.py:325
  11.5 2.5 %collective-permute-start.1 = (bf16[360,512]{1,0:T(8,128)(2,1)}, bf16[360,512]{1,0:T(8,128)(2,1)}, u32[]{:S(2)}, u32[]{:S(2)}) collective-permute-start(bf16[360,512]{1,0:T(8,128)(2,1)} %get-tuple-element.21), channel_id=1, source_target_pairs={{0,2},{1,3},{2,0},{3,1},{4,6},{5,7},{6,4},{7,5},{8,10},{9,11},{10,... | collective-permute-start | bytes 1105928 | tf_op jit(solution)/shard_map/ppermute | solution.py:318
  14.0 1.3 collective-permute-start.2
  16.2 7.8 %shard_map.114 = (bf16[4,768,360]{2,1,0:T(8,128)(2,1)S(1)}, bf16[2,360,768]{2,1,0:T(8,128)(2,1)S(1)}) custom-call(f32[768,2]{1,0:T(8,128)S(1)} %copy.31.down_ref, f32[2,768]{1,0:T(2,128)S(1)} %get-tuple-element.36.across_ref, bf16[8,360,256]{2,1,0:T(8,128)(2,1)S(1)} %shard_map.113.after_ref), custom_call_target="tpu_custom_call" | custom-call | bytes 1048576 | tf_op jit(solution)/shard_map/pallas_call | solution.py:22
  24.2 6.9 %collective-permute-done.refs_1_ = bf16[360,512]{1,0:T(8,128)(2,1)} collective-permute-done((bf16[360,512]{1,0:T(8,128)(2,1)}, bf16[360,512]{1,0:T(8,128)(2,1)}, u32[]{:S(2)}, u32[]{:S(2)}) %collective-permute-start) | collective-permute-done | bytes 368672 | tf_op jit(solution)/shard_map/ppermute | solution.py:318
  31.9 4.0 %shard_map.115 = bf16[3072,128]{1,0:T(8,128)(2,1)} custom-call(bf16[4,768,360]{2,1,0:T(8,128)(2,1)S(1)} %get-tuple-element.19.table_ref, bf16[360,512]{1,0:T(8,128)(2,1)S(1)} %get-tuple-element.18.after_ref.refs_0_, bf16[360,512]{1,0:T(8,128)(2,1)} %collective-permute-done.refs_1_, bf16[360,512]{1,0:T(8,128)(2,1)} %collective-permute-done.1.refs_2_, ...), custom_call_target="tpu_custom_call" | custom-call | bytes 1048576 | tf_op jit(solution)/shard_map/pallas_call | solution.py:22
  35.8 11.6 %all-to-all-start = ((bf16[64,48,128]{2,1,0:T(8,128)(2,1)}), bf16[64,48,128]{2,1,0:T(8,128)(2,1)S(1)}, u32[]{:S(2)}, u32[]{:S(2)}) async-start(bf16[64,48,128]{2,1,0:T(8,128)(2,1)} %bitcast.1), calls=%async_computation | async-start | bytes 1572864 | tf_op jit(solution)/shard_map/all_to_all | solution.py:424
  47.4 22.6 %all-to-all-done = bf16[64,48,128]{2,1,0:T(8,128)(2,1)S(1)} async-done(((bf16[64,48,128]{2,1,0:T(8,128)(2,1)}), bf16[64,48,128]{2,1,0:T(8,128)(2,1)S(1)}, u32[]{:S(2)}, u32[]{:S(2)}) %all-to-all-start) | async-done | bytes 786464 | tf_op jit(solution)/shard_map/all_to_all | solution.py:424
  70.0 1.7 copy-done.3
  71.7 6.2 %shard_map.116 = bf16[3072,128]{1,0:T(8,128)(2,1)} custom-call(bf16[6,512,384]{2,1,0:T(8,128)(2,1)S(1)} %copy-done.3, f32[6,1,384]{2,1,0:T(1,128)S(1)} %broadcast_in_dim.18.mask_ref, bf16[3072,128]{1,0:T(8,128)(2,1)S(1)} %bitcast.49), custom_call_target="tpu_custom_call" | custom-call | bytes 1048576 | tf_op jit(solution)/shard_map/pallas_call | solution.py:22
  77.9 6.4 %all-to-all-start.1 = ((bf16[64,48,128]{2,1,0:T(8,128)(2,1)}), bf16[64,48,128]{2,1,0:T(8,128)(2,1)S(1)}, u32[]{:S(2)}, u32[]{:S(2)}) async-start(bf16[64,48,128]{2,1,0:T(8,128)(2,1)} %bitcast.3), calls=%async_computation.1 | async-start | bytes 1572864 | tf_op jit(solution)/shard_map/all_to_all | solution.py:428
  84.7 22.3 %all-to-all-done.1 = bf16[64,48,128]{2,1,0:T(8,128)(2,1)S(1)} async-done(((bf16[64,48,128]{2,1,0:T(8,128)(2,1)}), bf16[64,48,128]{2,1,0:T(8,128)(2,1)S(1)}, u32[]{:S(2)}, u32[]{:S(2)}) %all-to-all-start.1) | async-done | bytes 786464 | tf_op jit(solution)/shard_map/all_to_all | solution.py:428
  107.0 1.2 collective-permute-start.5
  108.2 1.5 collective-permute-start.7
  109.7 2.2 %pad_maximum_fusion = bf16[24,360,256]{2,1,0:T(8,128)(2,1)S(1)} fusion(bf16[8,360,256]{2,1,0:T(8,128)(2,1)} %collective-permute-done.4, bf16[8,360,256]{2,1,0:T(8,128)(2,1)S(1)} %copy-done.2, bf16[8,360,256]{2,1,0:T(8,128)(2,1)} %collective-permute-done.3), kind=kLoop, calls=%fused_computation | loop fusion | flops 4423680 | bytes 8847360 | tf_op jit(solution)/shard_map/concatenate | solution.py:331
  111.9 1.3 fusion.6
  113.3 1.3 fusion.9
  114.9 1.3 fusion.12
  116.3 3.0 %collective-permute-start.10 = (bf16[8,1,256]{2,0,1:T(8,128)(2,1)S(1)}, bf16[8,1,256]{2,0,1:T(8,128)(2,1)S(1)}, u32[]{:S(2)}, u32[]{:S(2)}) collective-permute-start(bf16[8,1,256]{2,0,1:T(8,128)(2,1)S(1)} %slice.67), channel_id=1, source_target_pairs={{0,3},{1,0},{2,1},{3,2},{4,7},{5,4},{6,5},{7,6},{8,11},{9,8},{10,9... | collective-permute-start | bytes 12296 | tf_op jit(solution)/shard_map/ppermute | solution.py:318
  119.8 6.5 %collective-permute-done.9 = bf16[8,1,256]{2,0,1:T(8,128)(2,1)S(1)} collective-permute-done((bf16[8,1,256]{2,0,1:T(8,128)(2,1)S(1)}, bf16[8,1,256]{2,0,1:T(8,128)(2,1)S(1)}, u32[]{:S(2)}, u32[]{:S(2)}) %collective-permute-start.9) | collective-permute-done | bytes 4128 | tf_op jit(solution)/shard_map/ppermute | solution.py:318
  126.8 1.0 slice-done.1
  129.6 2.7 %collective-permute-start.8 = (bf16[1536,128]{1,0:T(8,128)(2,1)S(1)}, bf16[1536,128]{1,0:T(8,128)(2,1)S(1)}, u32[]{:S(2)}, u32[]{:S(2)}) collective-permute-start(bf16[1536,128]{1,0:T(8,128)(2,1)S(1)} %slice.60), channel_id=1, source_target_pairs={{0,3},{1,0},{2,1},{3,2},{4,7},{5,4},{6,5},{7,6},{8,11},{9,8},{10,9... | collective-permute-start | bytes 1179656 | tf_op jit(solution)/shard_map/ppermute | solution.py:318
  132.9 6.5 %collective-permute-done.6.far_west_ref = bf16[1536,128]{1,0:T(8,128)(2,1)S(1)} collective-permute-done((bf16[1536,128]{1,0:T(8,128)(2,1)S(1)}, bf16[1536,128]{1,0:T(8,128)(2,1)S(1)}, u32[]{:S(2)}, u32[]{:S(2)}) %collective-permute-start.6) | collective-permute-done | bytes 393248 | tf_op jit(solution)/shard_map/ppermute | solution.py:318
  139.5 9.3 %shard_map.117 = (bf16[4,720,256]{2,1,0:T(8,128)(2,1)}, bf16[1280,256]{1,0:T(8,128)(2,1)S(1)}) custom-call(bf16[3072,128]{1,0:T(8,128)(2,1)S(1)} %bitcast.52, bf16[3072,128]{1,0:T(8,128)(2,1)S(1)} %collective-permute-done.5.west_ref, bf16[1536,128]{1,0:T(8,128)(2,1)S(1)} %collective-permute-done.6.far_west_ref, ...), custom_call_target="tpu_custom_call" | custom-call | bytes 1048576 | tf_op jit(solution)/shard_map/pallas_call | solution.py:22
  148.8 20.7 %all_to_all.25 = bf16[32,40,256]{2,1,0:T(8,128)(2,1)S(1)} all-to-all(bf16[32,40,256]{2,1,0:T(8,128)(2,1)S(1)} %bitcast.54), channel_id=1, replica_groups={{0,1,2,3,4,5,6,7,8,9,10,11,12,13,14,15,16,17,18,19,20,21,22,23,24,25,26..., dimensions={0} | all-to-all | bytes 1310720 | tf_op jit(solution)/shard_map/all_to_all | solution.py:362
  169.6 11.9 %all_to_all.26 = bf16[8,40,256]{2,1,0:T(8,128)(2,1)S(1)} all-to-all(bf16[8,40,256]{2,1,0:T(8,128)(2,1)S(1)} %broadcast_in_dim.19), channel_id=1, replica_groups={{0,32,64,96,128,160,192,224},{4,36,68,100,132,164,196,228},{8,40,72,104..., dimensions={0} | all-to-all | bytes 327680 | tf_op jit(solution)/shard_map/all_to_all | solution.py:371
  181.5 18.5 %all_to_all.27 = bf16[32,40,256]{2,1,0:T(8,128)(2,1)S(1)} all-to-all(bf16[32,40,256]{2,1,0:T(8,128)(2,1)S(1)} %broadcast_in_dim.20), channel_id=1, replica_groups={{0,1,2,3,4,5,6,7,8,9,10,11,12,13,14,15,16,17,18,19,20,21,22,23,24,25,26..., dimensions={0} | all-to-all | bytes 1310720 | tf_op jit(solution)/shard_map/all_to_all | solution.py:380
  200.2 0.9 slice.69
  201.1 0.8 slice.68
  (74 shorter events, 6.6 us)
Async XLA Ops:
  0.6 83.7 %copy-start = (bf16[3,8,3,8]{3,1,2,0:T(8,128)(2,1)S(1)}, bf16[3,8,3,8]{3,1,2,0:T(8,128)(2,1)}, u32[]{:S(2)}) copy-start(bf16[3,8,3,8]{3,1,2,0:T(8,128)(2,1)} %param.15) | copy-start | bytes 3460
  0.6 1.4 copy-start.1
  3.6 11.7 %copy-start.9 = (s32[384]{0:T(512)S(1)}, s32[384]{0:T(512)}, u32[]{:S(2)}) copy-start(s32[384]{0:T(512)} %param.13) | copy-start | bytes 4612
  3.6 12.4 %copy-start.10 = (f32[8]{0:T(128)S(1)}, f32[8]{0:T(128)}, u32[]{:S(2)}) copy-start(f32[8]{0:T(128)} %param.12) | copy-start | bytes 100
  3.7 32.1 %collective-permute-start.3 = (bf16[8,360,256]{2,1,0:T(8,128)(2,1)S(1)}, bf16[8,360,256]{2,1,0:T(8,128)(2,1)}, u32[]{:S(2)}, u32[]{:S(2)}) collective-permute-start(bf16[8,360,256]{2,1,0:T(8,128)(2,1)S(1)} %shard_map.113.after_ref), channel_id=1, source_target_pairs={{0,4},{4,8},{8,12},{12,16},{16,20},{20,24},{24,28},{28,32},{32,36}... | collective-permute-start | bytes 4423688 | tf_op jit(solution)/shard_map/ppermute | solution.py:325
  8.3 27.5 %collective-permute-start.4 = (bf16[8,360,256]{2,1,0:T(8,128)(2,1)S(1)}, bf16[8,360,256]{2,1,0:T(8,128)(2,1)}, u32[]{:S(2)}, u32[]{:S(2)}) collective-permute-start(bf16[8,360,256]{2,1,0:T(8,128)(2,1)S(1)} %shard_map.113.after_ref), channel_id=1, source_target_pairs={{4,0},{8,4},{12,8},{16,12},{20,16},{24,20},{28,24},{32,28},{36,32}... | collective-permute-start | bytes 4423688 | tf_op jit(solution)/shard_map/ppermute | solution.py:325
  11.2 19.8 %collective-permute-start = (bf16[360,512]{1,0:T(8,128)(2,1)}, bf16[360,512]{1,0:T(8,128)(2,1)}, u32[]{:S(2)}, u32[]{:S(2)}) collective-permute-start(bf16[360,512]{1,0:T(8,128)(2,1)} %get-tuple-element.20), channel_id=1, source_target_pairs={{0,1},{1,2},{2,3},{3,0},{4,5},{5,6},{6,7},{7,4},{8,9},{9,10},{10,1... | collective-permute-start | bytes 1105928 | tf_op jit(solution)/shard_map/ppermute | solution.py:318
  11.5 19.5 %collective-permute-start.1 = (bf16[360,512]{1,0:T(8,128)(2,1)}, bf16[360,512]{1,0:T(8,128)(2,1)}, u32[]{:S(2)}, u32[]{:S(2)}) collective-permute-start(bf16[360,512]{1,0:T(8,128)(2,1)} %get-tuple-element.21), channel_id=1, source_target_pairs={{0,2},{1,3},{2,0},{3,1},{4,6},{5,7},{6,4},{7,5},{8,10},{9,11},{10,... | collective-permute-start | bytes 1105928 | tf_op jit(solution)/shard_map/ppermute | solution.py:318
  14.0 17.9 %collective-permute-start.2 = (bf16[360,512]{1,0:T(8,128)(2,1)}, bf16[360,512]{1,0:T(8,128)(2,1)}, u32[]{:S(2)}, u32[]{:S(2)}) collective-permute-start(bf16[360,512]{1,0:T(8,128)(2,1)} %get-tuple-element.22), channel_id=1, source_target_pairs={{0,3},{1,0},{2,1},{3,2},{4,7},{5,4},{6,5},{7,6},{8,11},{9,8},{10,9... | collective-permute-start | bytes 1105928 | tf_op jit(solution)/shard_map/ppermute | solution.py:318
  35.8 34.2 %all-to-all-start = ((bf16[64,48,128]{2,1,0:T(8,128)(2,1)}), bf16[64,48,128]{2,1,0:T(8,128)(2,1)S(1)}, u32[]{:S(2)}, u32[]{:S(2)}) async-start(bf16[64,48,128]{2,1,0:T(8,128)(2,1)} %bitcast.1), calls=%async_computation | async-start | bytes 1572864 | tf_op jit(solution)/shard_map/all_to_all | solution.py:424
  70.0 1.7 copy-start.3
  77.8 6.4 %copy-start.11 = (s32[1,3]{1,0:T(1,128)S(1)}, s32[1,3]{1,0:T(1,128)}, u32[]{:S(2)}) copy-start(s32[1,3]{1,0:T(1,128)} %param.14) | copy-start | bytes 40
  77.9 31.8 %copy-start.2 = (bf16[8,360,256]{2,1,0:T(8,128)(2,1)S(1)}, bf16[8,360,256]{2,1,0:T(8,128)(2,1)}, u32[]{:S(2)}) copy-start(bf16[8,360,256]{2,1,0:T(8,128)(2,1)} %value_ref.1) | copy-start | bytes 4423684
  77.9 29.1 %all-to-all-start.1 = ((bf16[64,48,128]{2,1,0:T(8,128)(2,1)}), bf16[64,48,128]{2,1,0:T(8,128)(2,1)S(1)}, u32[]{:S(2)}, u32[]{:S(2)}) async-start(bf16[64,48,128]{2,1,0:T(8,128)(2,1)} %bitcast.3), calls=%async_computation.1 | async-start | bytes 1572864 | tf_op jit(solution)/shard_map/all_to_all | solution.py:428
  107.0 22.4 %collective-permute-start.5 = (bf16[3072,128]{1,0:T(8,128)(2,1)S(1)}, bf16[3072,128]{1,0:T(8,128)(2,1)S(1)}, u32[]{:S(2)}, u32[]{:S(2)}) collective-permute-start(bf16[3072,128]{1,0:T(8,128)(2,1)S(1)} %bitcast.50), channel_id=1, source_target_pairs={{0,1},{1,2},{2,3},{3,0},{4,5},{5,6},{6,7},{7,4},{8,9},{9,10},{10,1... | collective-permute-start | bytes 2359304 | tf_op jit(solution)/shard_map/ppermute | solution.py:318
  108.2 21.4 %collective-permute-start.7 = (bf16[3072,128]{1,0:T(8,128)(2,1)S(1)}, bf16[3072,128]{1,0:T(8,128)(2,1)S(1)}, u32[]{:S(2)}, u32[]{:S(2)}) collective-permute-start(bf16[3072,128]{1,0:T(8,128)(2,1)S(1)} %bitcast.51), channel_id=1, source_target_pairs={{0,3},{1,0},{2,1},{3,2},{4,7},{5,4},{6,5},{7,6},{8,11},{9,8},{10,9... | collective-permute-start | bytes 2359304 | tf_op jit(solution)/shard_map/ppermute | solution.py:318
  113.2 6.6 %copy-start.6 = (bf16[8,360,256]{2,0,1:T(8,128)(2,1)}, bf16[8,360,256]{2,0,1:T(8,128)(2,1)S(1)}, u32[]{:S(2)}) copy-start(bf16[8,360,256]{2,0,1:T(8,128)(2,1)S(1)} %fusion.6) | copy-start | bytes 4423684
  113.2 13.1 %collective-permute-start.9 = (bf16[8,1,256]{2,0,1:T(8,128)(2,1)S(1)}, bf16[8,1,256]{2,0,1:T(8,128)(2,1)S(1)}, u32[]{:S(2)}, u32[]{:S(2)}) collective-permute-start(bf16[8,1,256]{2,0,1:T(8,128)(2,1)S(1)} %slice.62), channel_id=1, source_target_pairs={{0,1},{1,2},{2,3},{3,0},{4,5},{5,6},{6,7},{7,4},{8,9},{9,10},{10,1... | collective-permute-start | bytes 12296 | tf_op jit(solution)/shard_map/ppermute | solution.py:318
  114.9 4.3 %copy-start.8 = (bf16[3,256,256]{2,1,0:T(8,128)(2,1)S(1)}, bf16[3,256,256]{2,1,0:T(8,128)(2,1)}, u32[]{:S(2)}) copy-start(bf16[3,256,256]{2,1,0:T(8,128)(2,1)} %param.17) | copy-start | bytes 1179652
  116.3 3.6 %copy-start.7 = (bf16[8,360,256]{2,0,1:T(8,128)(2,1)}, bf16[8,360,256]{2,0,1:T(8,128)(2,1)S(1)}, u32[]{:S(2)}) copy-start(bf16[8,360,256]{2,0,1:T(8,128)(2,1)S(1)} %fusion.12) | copy-start | bytes 4423684
  116.3 10.6 %collective-permute-start.10 = (bf16[8,1,256]{2,0,1:T(8,128)(2,1)S(1)}, bf16[8,1,256]{2,0,1:T(8,128)(2,1)S(1)}, u32[]{:S(2)}, u32[]{:S(2)}) collective-permute-start(bf16[8,1,256]{2,0,1:T(8,128)(2,1)S(1)} %slice.67), channel_id=1, source_target_pairs={{0,3},{1,0},{2,1},{3,2},{4,7},{5,4},{6,5},{7,6},{8,11},{9,8},{10,9... | collective-permute-start | bytes 12296 | tf_op jit(solution)/shard_map/ppermute | solution.py:318
  119.8 6.5 %slice-start = ((bf16[8,360,256]{2,0,1:T(8,128)(2,1)}), bf16[8,359,256]{2,0,1:T(8,128)(2,1)S(1)}, s32[]{:S(2)}) async-start(bf16[8,360,256]{2,0,1:T(8,128)(2,1)} %copy-done.6), calls=%async_computation.5 | async-start | bytes 2940928 | tf_op jit(solution)/shard_map/slice | solution.py:347
  126.5 1.4 slice-start.1
  129.5 10.0 %collective-permute-start.6 = (bf16[1536,128]{1,0:T(8,128)(2,1)S(1)}, bf16[1536,128]{1,0:T(8,128)(2,1)S(1)}, u32[]{:S(2)}, u32[]{:S(2)}) collective-permute-start(bf16[1536,128]{1,0:T(8,128)(2,1)S(1)} %slice.59), channel_id=1, source_target_pairs={{0,1},{1,2},{2,3},{3,0},{4,5},{5,6},{6,7},{7,4},{8,9},{9,10},{10,1... | collective-permute-start | bytes 1179656 | tf_op jit(solution)/shard_map/ppermute | solution.py:318
  129.6 9.9 %collective-permute-start.8 = (bf16[1536,128]{1,0:T(8,128)(2,1)S(1)}, bf16[1536,128]{1,0:T(8,128)(2,1)S(1)}, u32[]{:S(2)}, u32[]{:S(2)}) collective-permute-start(bf16[1536,128]{1,0:T(8,128)(2,1)S(1)} %slice.60), channel_id=1, source_target_pairs={{0,3},{1,0},{2,1},{3,2},{4,7},{5,4},{6,5},{7,6},{8,11},{9,8},{10,9... | collective-permute-start | bytes 1179656 | tf_op jit(solution)/shard_map/ppermute | solution.py:318
  132.3 7.1 %copy-start.4 = (bf16[8,360,256]{2,1,0:T(8,128)(2,1)S(1)}, bf16[8,360,256]{2,1,0:T(8,128)(2,1)}, u32[]{:S(2)}) copy-start(bf16[8,360,256]{2,1,0:T(8,128)(2,1)} %param.10) | copy-start | bytes 4423684
  132.3 7.2 %copy-start.5 = (bf16[2,256,256]{2,1,0:T(8,128)(2,1)S(1)}, bf16[2,256,256]{2,1,0:T(8,128)(2,1)}, u32[]{:S(2)}) copy-start(bf16[2,256,256]{2,1,0:T(8,128)(2,1)} %param.16) | copy-start | bytes 786436
